TPU v7x, 512 devices: a whole 4x4x16 slice. The times are simulated.
512 devices in a mesh: row: 32 (over y, x, core), col: 16 (over z).
Axes of the slice: x: 4, y: 4, z: 16, core: 2. Of those that a mesh axis runs over, the one named last changes fastest.
Arguments:
- nodes: bfloat16 [65536, 128], P(('row', 'col')), may hold values from -6 to 6
- edges: bfloat16 [1572864, 128], P(('row', 'col')), may hold values from -6 to 6
- send_list: int32 [8192, 32], P(('row', 'col')), may hold values from 0 to 127, as said below
- recv_list: int32 [16384, 16], P(('row', 'col')), may hold values from 0 to 127, as said below
- sender_slot: int32 [12288, 128], P(('row', 'col')), may hold values from 0 to 511
- receiver_slot: int32 [12288, 128], P(('row', 'col')), may hold values from 0 to 511
- tile_count: int32 [12288], P(('row', 'col')), may hold values from 0 to 128, as said below
- edge_in_weight: bfloat16 [384, 128], replicated, may hold values from -0.3125 to 0.3125
- edge_out_weight: bfloat16 [2, 128, 128], replicated, may hold values from -0.5 to 0.5
- edge_bias: float32 [3, 128], replicated, may hold values from -3 to 3
- edge_gain: float32 [128], replicated, may hold values from 0.1 to 1.9
- edge_shift: float32 [128], replicated, may hold values from -3 to 3
- node_in_weight: bfloat16 [256, 128], replicated, may hold values from -0.375 to 0.375
- node_out_weight: bfloat16 [2, 128, 128], replicated, may hold values from -0.5 to 0.5
- node_bias: float32 [3, 128], replicated, may hold values from -3 to 3
- node_gain: float32 [128], replicated, may hold values from 0.1 to 1.9
- node_shift: float32 [128], replicated, may hold values from -3 to 3
Outputs:
- new_nodes: bfloat16 [65536, 128], P(('row', 'col'))
- new_edges: bfloat16 [1572864, 128], P(('row', 'col'))
Inputs may be any that keep to these rules, and one draw needn't show every extreme that they name: `send_list`: within one row of the list the entries are distinct. `recv_list`: within one row of the list the entries are distinct. `tile_count`: on every device the tiles with count 0 come after all tiles with a nonzero count, and at least one tile has a nonzero count; all tiles before a device's last nonzero one hold 128; some device has all 24 tiles at 128.
All inputs are finite; a program needn't handle non-finite values.
Results may differ from a plain program's by a relative error of at most 0.015.
Values may be sent and summed in bfloat16 or wider, within the bound.
No kernel may reach another device: no remote copies, remote signals or barrier semaphores. Data moves between devices by JAX's collectives and lax.ppermute only.
A program may use at most 64 MiB of HBM per device.

v0:
```python
import jax
import jax.numpy as jnp
from jax import lax
from jax.sharding import PartitionSpec as P


def layer_norm(values, gain, shift):
    mean = jnp.mean(values, axis=-1, keepdims=True)
    centred = values - mean
    spread = jnp.mean(centred * centred, axis=-1, keepdims=True)
    return centred * lax.rsqrt(spread + 1e-05) * gain + shift


def perceptron(inputs, w_in, w_out, biases, gain, shift):
    hidden = jnp.maximum(
        jnp.dot(inputs, w_in, preferred_element_type=jnp.float32) + biases[0], 0.0
    ).astype(jnp.bfloat16)
    hidden = jnp.maximum(
        jnp.dot(hidden, w_out[0], preferred_element_type=jnp.float32) + biases[1], 0.0
    ).astype(jnp.bfloat16)
    output = jnp.dot(hidden, w_out[1], preferred_element_type=jnp.float32) + biases[2]
    return layer_norm(output, gain, shift)


def block_rows(lists, node_rows):
    peers, depth = lists.shape
    owner = lax.broadcasted_iota(jnp.int32, (peers, depth), 0)
    return (owner * node_rows + lists).reshape(-1)


def local(
    nodes,
    edges,
    send_list,
    recv_list,
    sender_slot,
    receiver_slot,
    tile_count,
    edge_in_weight,
    edge_out_weight,
    edge_bias,
    edge_gain,
    edge_shift,
    node_in_weight,
    node_out_weight,
    node_bias,
    node_gain,
    node_shift,
):
    node_rows, width = nodes.shape
    tiles, tile = sender_slot.shape
    edge_tiles = edges.reshape(tiles, tile, width)
    send_block = lax.all_gather(nodes, "col", axis=0, tiled=True)
    recv_block = lax.all_gather(nodes, "row", axis=0, tiled=True)
    send_pick = block_rows(send_list, node_rows)
    recv_pick = block_rows(recv_list, node_rows)
    send_table = jnp.take(send_block, send_pick, axis=0)
    recv_table = jnp.take(recv_block, recv_pick, axis=0)
    send_width = send_table.shape[0]
    recv_width = recv_table.shape[0]
    busy_tiles = jnp.sum((tile_count > 0).astype(jnp.int32))

    def tile_step(step, state):
        new_buffer, send_part, recv_part = state
        edge_feat = lax.dynamic_index_in_dim(edge_tiles, step, 0, keepdims=False)
        send_rows = lax.dynamic_index_in_dim(sender_slot, step, 0, keepdims=False)
        recv_rows = lax.dynamic_index_in_dim(receiver_slot, step, 0, keepdims=False)
        send_hot = (
            send_rows[:, None] == lax.broadcasted_iota(jnp.int32, (tile, send_width), 1)
        ).astype(jnp.bfloat16)
        recv_hot = (
            recv_rows[:, None] == lax.broadcasted_iota(jnp.int32, (tile, recv_width), 1)
        ).astype(jnp.bfloat16)
        send_feat = jnp.dot(send_hot, send_table, preferred_element_type=jnp.float32).astype(
            jnp.bfloat16
        )
        recv_feat = jnp.dot(recv_hot, recv_table, preferred_element_type=jnp.float32).astype(
            jnp.bfloat16
        )
        joined = jnp.concatenate([edge_feat, send_feat, recv_feat], axis=1)
        update = perceptron(
            joined, edge_in_weight, edge_out_weight, edge_bias, edge_gain, edge_shift
        )
        valid = lax.broadcasted_iota(jnp.int32, (tile, 1), 0) < tile_count[step]
        fresh = jnp.where(
            valid, edge_feat.astype(jnp.float32) + update, jnp.zeros_like(update)
        ).astype(jnp.bfloat16)
        new_buffer = lax.dynamic_update_index_in_dim(new_buffer, fresh, step, 0)
        send_part = send_part + lax.dot_general(
            send_hot, fresh, (((0,), (0,)), ((), ())), preferred_element_type=jnp.float32
        )
        recv_part = recv_part + lax.dot_general(
            recv_hot, fresh, (((0,), (0,)), ((), ())), preferred_element_type=jnp.float32
        )
        return (new_buffer, send_part, recv_part)

    start_state = (
        jnp.zeros((tiles, tile, width), jnp.bfloat16),
        jnp.zeros((send_width, width), jnp.float32),
        jnp.zeros((recv_width, width), jnp.float32),
    )
    new_buffer, send_part, recv_part = lax.fori_loop(0, busy_tiles, tile_step, start_state)
    send_full = jnp.zeros((send_block.shape[0], width), jnp.float32).at[send_pick].add(send_part)
    recv_full = jnp.zeros((recv_block.shape[0], width), jnp.float32).at[recv_pick].add(recv_part)
    total = lax.psum_scatter(
        send_full.astype(jnp.bfloat16), "col", scatter_dimension=0, tiled=True
    ).astype(jnp.float32) + lax.psum_scatter(
        recv_full.astype(jnp.bfloat16), "row", scatter_dimension=0, tiled=True
    ).astype(
        jnp.float32
    )
    joined_nodes = jnp.concatenate([nodes, total.astype(jnp.bfloat16)], axis=1)
    node_update = perceptron(
        joined_nodes, node_in_weight, node_out_weight, node_bias, node_gain, node_shift
    )
    new_nodes = (nodes.astype(jnp.float32) + node_update).astype(jnp.bfloat16)
    return (new_nodes, new_buffer.reshape(tiles * tile, width))


def solution(mesh):
    placed = (
        P(("row", "col"), None),
        P(("row", "col"), None),
        P(("row", "col"), None),
        P(("row", "col"), None),
        P(("row", "col"), None),
        P(("row", "col"), None),
        P(("row", "col")),
        P(),
        P(),
        P(),
        P(),
        P(),
        P(),
        P(),
        P(),
        P(),
        P(),
    )
    return jax.shard_map(
        local,
        mesh=mesh,
        in_specs=placed,
        out_specs=(P(("row", "col"), None), P(("row", "col"), None)),
        check_vma=False,
    )
```

profile of v0, /device:TPU:1, one launch (start us, length us, event | category | flops | bytes accessed | tf_op | source)
XLA Modules:
  0.0 395.2 jit_solution(13108384275549389138)
XLA Ops:
  7.2 0.0 copy-start
  7.2 0.0 all-gather.2.cloned.1.call-start
  7.2 0.7 all-gather.2.cloned.1.call-update
  7.9 0.0 reduce-scatter.3.cloned.1.call-start
  8.0 0.8 broadcast_add_fusion.1
  8.7 0.1 reshape.127
  8.8 0.1 reshape.125
  8.9 0.7 broadcast_add_fusion
  9.6 0.1 copy.23
  9.7 0.1 reshape.129
  9.8 0.1 reshape.128
  9.9 32.1 %all_gather.6 = bf16[2048,128]{1,0:T(8,128)(2,1)S(1)} all-gather(bf16[128,128]{1,0:T(8,128)(2,1)} %param.19), channel_id=1, replica_groups=mesh['row'=32,'col'=16] {'col'}, dimensions={0}, use_global_device_ids=true | all-gather | bytes 557056 | tf_op jit(solution)/shard_map/all_gather | solution.py:53
  41.9 0.0 copy-start.11
  42.0 0.0 copy-start.12
  42.0 1.3 gather_fusion
  43.3 1.3 fusion.53
  44.7 0.1 broadcast_select_fusion.1
  44.8 30.2 %all-gather.2.cloned.1.call-done = bf16[4096,128]{1,0:T(8,128)(2,1)} async-done(((bf16[128,128]{1,0:T(8,128)(2,1)}), bf16[4096,128]{1,0:T(8,128)(2,1)}) %all-gather.2.cloned.1.call-update) | async-done | bytes 1048592 | tf_op jit(solution)/shard_map/all_gather | solution.py:54
  75.0 2.4 gather_fusion.1
  77.4 0.1 broadcast_select_fusion
  77.6 0.2 broadcast_in_dim.52.clone
  77.8 0.0 copy-done.2
  77.8 0.0 copy-done.4
  77.8 0.0 copy-done.6
  77.8 0.0 copy-done.7
  77.8 0.0 copy-done.11
  77.8 0.0 copy-done.12
  77.8 6.3 %while.14 = (s32[]{:T(128)}, bf16[24,128,128]{2,1,0:T(8,128)(2,1)S(1)}, f32[512,128]{1,0:T(8,128)S(1)}, f32[512,128]{1,0:T(8,128)S(1)}, s32[]{:T(128)}, /*index=...) while((s32[]{:T(128)}, ...), condition=%wide.region_4.5_spmd, body=%wide.region_1.0_spmd.sunk | while | flops 89243904 | bytes 2308595 | solution.py:102
  78.5 0.6 dynamic_slice.26
  79.1 0.6 iota_compare_fusion.10
  79.8 0.7 fusion.90
  80.5 0.3 convolution_convert_fusion.4
  80.8 0.3 convolution_convert_fusion.5
  81.0 0.8 constant_dynamic-slice_fusion.4
  81.8 0.1 copy.33
  81.9 0.4 fusion.91
  82.3 0.2 fusion.92
  82.6 0.1 select_convert_fusion.2
  82.7 0.1 copy.34
  82.8 0.3 convolution_add_fusion.11
  83.1 0.3 convolution_add_fusion.10
  84.1 0.0 copy-start.1
  84.1 2.5 scatter_custom_fusion
  86.6 0.9 convert_element_type.52
  87.5 0.0 reduce-scatter.3.cloned.1.call-update
  87.5 0.0 reduce-scatter.5.cloned.1.call-start
  87.6 2.8 scatter_custom_fusion.1
  90.3 0.0 copy-done.1
  90.3 0.0 copy-start.3
  90.4 0.0 copy-start.8
  90.4 0.0 copy-start.5
  90.4 0.0 copy-start.9
  90.4 0.0 copy-start.10
  90.4 1.1 convert_element_type.54
  91.5 0.0 reduce-scatter.5.cloned.1.call-update
  91.5 0.0 copy-done.3
  91.5 0.1 copy.22
  91.7 181.8 %reduce-scatter.3.cloned.1.call-done = bf16[128,128]{1,0:T(8,128)(2,1)} async-done(((bf16[2048,128]{1,0:T(8,128)(2,1)}), bf16[128,128]{1,0:T(8,128)(2,1)}) %reduce-scatter.3.cloned.1.call-update) | async-done | bytes 32784 | tf_op jit(solution)/shard_map/reduce_scatter | solution.py:105
  273.4 113.0 %reduce-scatter.5.cloned.1.call-done = bf16[128,128]{1,0:T(8,128)(2,1)} async-done(((bf16[4096,128]{1,0:T(8,128)(2,1)}), bf16[128,128]{1,0:T(8,128)(2,1)}) %reduce-scatter.5.cloned.1.call-update) | async-done | bytes 32784 | tf_op jit(solution)/shard_map/reduce_scatter | solution.py:107
  386.4 0.8 add_convert_fusion.1
  387.2 0.3 fusion.36
  387.5 0.2 fusion.58
  387.8 0.1 add_convert_fusion
  387.9 0.7 copy.27
  (28 shorter events, 0.2 us)
Async XLA Ops:
  7.2 380.0 %copy-start = (bf16[256,128]{1,0:T(8,128)(2,1)S(1)}, bf16[256,128]{1,0:T(8,128)(2,1)}, u32[]{:S(2)}) copy-start(bf16[256,128]{1,0:T(8,128)(2,1)} %param.31) | copy-start | bytes 196612
  7.2 67.8 %all-gather.2.cloned.1.call-start = ((), (), s32[]{:S(2)}) async-start(), calls=%async_computation.2 | async-start | bytes 1081344 | tf_op jit(solution)/shard_map/all_gather | solution.py:54
  7.9 265.5 %reduce-scatter.3.cloned.1.call-start = ((), (), s32[]{:S(2)}) async-start(), calls=%async_computation.3 | async-start | bytes 557056 | tf_op jit(solution)/shard_map/reduce_scatter | solution.py:105
  41.9 35.9 %copy-start.2 = (bf16[2,128,128]{2,1,0:T(8,128)(2,1)S(1)}, bf16[2,128,128]{2,1,0:T(8,128)(2,1)}, u32[]{:S(2)}) copy-start(bf16[2,128,128]{2,1,0:T(8,128)(2,1)} %param.27) | copy-start | bytes 196612
  41.9 35.9 %copy-start.4 = (f32[3,128]{1,0:T(4,128)S(1)}, f32[3,128]{1,0:T(4,128)}, u32[]{:S(2)}) copy-start(f32[3,128]{1,0:T(4,128)} %param.28) | copy-start | bytes 4612
  41.9 35.9 %copy-start.6 = (f32[128]{0:T(128)S(1)}, f32[128]{0:T(128)}, u32[]{:S(2)}) copy-start(f32[128]{0:T(128)} %param.29) | copy-start | bytes 1540
  41.9 35.9 %copy-start.7 = (f32[128]{0:T(128)S(1)}, f32[128]{0:T(128)}, u32[]{:S(2)}) copy-start(f32[128]{0:T(128)} %param.30) | copy-start | bytes 1540
  41.9 35.9 %copy-start.11 = (bf16[384,128]{1,0:T(8,128)(2,1)S(1)}, bf16[384,128]{1,0:T(8,128)(2,1)}, u32[]{:S(2)}) copy-start(bf16[384,128]{1,0:T(8,128)(2,1)} %param.26) | copy-start | bytes 294916
  42.0 35.9 %copy-start.12 = (s32[24]{0:T(128)S(1)}, s32[24]{0:T(128)}, u32[]{:S(2)}) copy-start(s32[24]{0:T(128)} %param.25) | copy-start | bytes 292
  84.1 6.2 %copy-start.1 = (bf16[24,128,128]{2,1,0:T(8,128)(2,1)}, bf16[24,128,128]{2,1,0:T(8,128)(2,1)S(1)}, u32[]{:S(2)}) copy-start(bf16[24,128,128]{2,1,0:T(8,128)(2,1)S(1)} %get-tuple-element.89) | copy-start | bytes 2359300
  87.5 298.9 %reduce-scatter.5.cloned.1.call-start = ((), (), s32[]{:S(2)}) async-start(), calls=%async_computation.4 | async-start | bytes 1081344 | tf_op jit(solution)/shard_map/reduce_scatter | solution.py:107
  90.3 1.2 copy-start.3
  90.4 1.3 copy-start.8
  90.4 296.8 %copy-start.5 = (bf16[2,128,128]{2,1,0:T(8,128)(2,1)S(1)}, bf16[2,128,128]{2,1,0:T(8,128)(2,1)}, u32[]{:S(2)}) copy-start(bf16[2,128,128]{2,1,0:T(8,128)(2,1)} %param.32) | copy-start | bytes 196612
  90.4 297.4 %copy-start.9 = (f32[128]{0:T(128)S(1)}, f32[128]{0:T(128)}, u32[]{:S(2)}) copy-start(f32[128]{0:T(128)} %param.35) | copy-start | bytes 1540
  90.4 297.4 %copy-start.10 = (f32[128]{0:T(128)S(1)}, f32[128]{0:T(128)}, u32[]{:S(2)}) copy-start(f32[128]{0:T(128)} %param.34) | copy-start | bytes 1540
Sparse Core Ops, SparseCore 0:
  11.1 63.8 all-gather.1
  87.6 185.7 reduce-scatter.2
  278.4 107.9 reduce-scatter.4
where the time goes:
time: 399 us; the launch traced here: 395 us
  waiting for transfers between devices  326 us (82%)
  blocking collectives  32.1 us (8%)
  between operations  14.1 us (4%)
  other arithmetic  12 us (3%)
  local copies, waits for them, and re-layouts  7.59 us (2%)
    reduce_scatter x1, waiting for transfers between devices, local(): lax.psum_scatter(send_full.astype(jnp.bfloat16), 'col', scatter_dimension...  182 us
    reduce_scatter x1, waiting for transfers between devices, local(): lax.psum_scatter(recv_full.astype(jnp.bfloat16), 'row', scatter_dimension...  113 us
    all_gather x1, blocking collectives, local(): send_block = lax.all_gather(nodes, 'col', axis=0, tiled=True)  32.1 us
    all_gather x1, waiting for transfers between devices, local(): recv_block = lax.all_gather(nodes, 'row', axis=0, tiled=True)  30.2 us
  transfers between devices with their start and end apart: 3, of which 3 were waited for; matrix products, arithmetic and copies ran while one was open for 2% of the time, Pallas kernels for 0%

commit v1 on v0

v1 whole, which is shorter than its diff:
```python
import jax
import jax.numpy as jnp
from jax import lax
from jax.experimental import pallas as pl
from jax.experimental.pallas import tpu as pltpu
from jax.sharding import PartitionSpec as P

F32 = jnp.float32
BF16 = jnp.bfloat16
EXTRA = 16
VMEM = pl.BlockSpec(memory_space=pltpu.VMEM)
SMEM = pl.BlockSpec(memory_space=pltpu.SMEM)
NN = (((1,), (0,)), ((), ()))
NT = (((1,), (1,)), ((), ()))
TN = (((0,), (0,)), ((), ()))


def mm(a, b, dims=NN):
    return lax.dot_general(a, b, dims, preferred_element_type=F32)


def repeat_lanes(lists, width):
    depth = lists.shape[1]
    place = (
        lax.broadcasted_iota(jnp.int32, (depth, width), 1) % depth
        == lax.broadcasted_iota(jnp.int32, (depth, width), 0)
    )
    return mm(lists.astype(F32).astype(BF16), place.astype(F32).astype(BF16))


def pack_kernel(nodes_ref, send_list_ref, recv_list_ref, row_ref, col_ref):
    rows, width = nodes_ref.shape
    peers = recv_list_ref.shape[0]
    col_ref[0:rows, :] = nodes_ref[...]
    col_ref[rows : rows + EXTRA, :] = repeat_lanes(send_list_ref[...], width).astype(BF16)
    recv_lanes = repeat_lanes(recv_list_ref[...], width)
    for peer in range(peers):
        row_ref[peer, 0:rows, :] = nodes_ref[...]
        row_ref[peer, rows : rows + EXTRA, :] = jnp.broadcast_to(
            recv_lanes[peer : peer + 1, :], (EXTRA, width)
        ).astype(BF16)


def merge_lists(picked, depth):
    peers, width = picked.shape
    per = width // depth
    lane_block = lax.broadcasted_iota(jnp.int32, (peers, width), 1) // depth
    own = lax.broadcasted_iota(jnp.int32, (peers, width), 0) % per
    kept = jnp.where(lane_block == own, picked, 0.0)
    return [
        jnp.sum(kept[j * per : (j + 1) * per, :], axis=0, keepdims=True)
        for j in range(peers // per)
    ]


def edge_kernel(
    count_ref,
    place_ref,
    row_ref,
    col_ref,
    send_list_ref,
    recv_list_ref,
    send_slot_ref,
    recv_slot_ref,
    edges_ref,
    w_in_ref,
    w_out_ref,
    bias_ref,
    gain_ref,
    shift_ref,
    new_ref,
    send_out_ref,
    recv_out_ref,
    owner_ref,
    send_acc,
    recv_acc,
):
    recv_peers, chunk, width = row_ref.shape
    send_peers = col_ref.shape[0]
    rows = chunk - EXTRA
    send_depth = send_list_ref.shape[1]
    recv_depth = recv_list_ref.shape[1]
    send_width = send_peers * send_depth
    recv_width = recv_peers * recv_depth
    tiles, tile = send_slot_ref.shape
    group = 4
    step_rows = group * tile

    me = place_ref[0]
    mine = lax.broadcasted_iota(jnp.int32, (EXTRA, width), 0) == me
    picked = [
        jnp.sum(
            jnp.where(mine, col_ref[p, rows : rows + EXTRA, :].astype(F32), 0.0),
            axis=0,
            keepdims=True,
        )
        for p in range(send_peers)
    ]
    send_owner = merge_lists(jnp.concatenate(picked, axis=0), send_depth)
    picked = [
        row_ref[p, rows : rows + EXTRA, :].astype(F32)[0:1, :] for p in range(recv_peers)
    ]
    recv_owner = merge_lists(jnp.concatenate(picked, axis=0), recv_depth)
    owner_ref[...] = jnp.concatenate(send_owner + recv_owner, axis=0)

    node_at = lax.broadcasted_iota(jnp.int32, (rows, 1), 0)

    def table(block_ref, list_ref, peers):
        parts = []
        for p in range(peers):
            hot = (node_at == list_ref[p : p + 1, :]).astype(F32).astype(BF16)
            parts.append(mm(hot, block_ref[p, 0:rows, :], TN))
        return jnp.concatenate(parts, axis=0).astype(BF16)

    send_table = table(col_ref, send_list_ref, send_peers)
    recv_table = table(row_ref, recv_list_ref, recv_peers)
    send_proj = mm(send_table, w_in_ref[width : 2 * width, :]).T.astype(BF16)
    recv_proj = mm(recv_table, w_in_ref[2 * width : 3 * width, :]).T.astype(BF16)
    edge_w = w_in_ref[0:width, :].astype(F32).T.astype(BF16)
    mid_w = w_out_ref[0].astype(F32).T.astype(BF16)
    last_w = w_out_ref[1].astype(F32).T.astype(BF16)
    columns = jnp.concatenate(
        [bias_ref[...], gain_ref[...], shift_ref[...], jnp.zeros((3, width), F32)], axis=0
    ).T
    b0, b1, b2 = columns[:, 0:1], columns[:, 1:2], columns[:, 2:3]
    gain, shift = columns[:, 3:4], columns[:, 4:5]

    send_at = lax.broadcasted_iota(jnp.int32, (send_width, tile), 0)
    recv_at = lax.broadcasted_iota(jnp.int32, (recv_width, tile), 0)
    row_at = lax.broadcasted_iota(jnp.int32, (tile, 1), 0)

    for step in range(tiles // group):
        first = step * group
        send_hot = jnp.concatenate(
            [
                (send_at == send_slot_ref[first + t : first + t + 1, :]).astype(F32).astype(BF16)
                for t in range(group)
            ],
            axis=1,
        )
        recv_hot = jnp.concatenate(
            [
                (recv_at == recv_slot_ref[first + t : first + t + 1, :]).astype(F32).astype(BF16)
                for t in range(group)
            ],
            axis=1,
        )
        edge = edges_ref[first * tile : first * tile + step_rows, :]
        hidden = mm(send_proj, send_hot) + mm(recv_proj, recv_hot) + mm(edge_w, edge, NT)
        hidden = jnp.maximum(hidden + b0, 0.0).astype(BF16)
        hidden = jnp.maximum(mm(mid_w, hidden) + b1, 0.0).astype(BF16)
        output = mm(last_w, hidden) + b2
        mean = jnp.sum(output, axis=0, keepdims=True) * (1.0 / width)
        centred = output - mean
        spread = jnp.sum(centred * centred, axis=0, keepdims=True) * (1.0 / width)
        update = (centred * lax.rsqrt(spread + 1e-05) * gain + shift).T
        valid = jnp.concatenate(
            [row_at < count_ref[first + t] for t in range(group)], axis=0
        )
        fresh = jnp.where(valid, edge.astype(F32) + update, 0.0).astype(BF16)
        new_ref[first * tile : first * tile + step_rows, :] = fresh
        send_sum = mm(send_hot, fresh)
        recv_sum = mm(recv_hot, fresh)
        if step == 0:
            send_acc[...] = send_sum
            recv_acc[...] = recv_sum
        else:
            send_acc[...] += send_sum
            recv_acc[...] += recv_sum
    send_out_ref[...] = send_acc[...].astype(BF16).reshape(send_out_ref.shape)
    recv_out_ref[...] = recv_acc[...].astype(BF16).reshape(recv_out_ref.shape)


def node_kernel(
    owner_ref,
    send_ref,
    recv_ref,
    nodes_ref,
    w_in_ref,
    w_out_ref,
    bias_ref,
    gain_ref,
    shift_ref,
    out_ref,
):
    rows, width = nodes_ref.shape
    send = send_ref[...].reshape(-1, width)
    recv = recv_ref[...].reshape(-1, width)
    node_at = lax.broadcasted_iota(jnp.int32, (rows, width), 0).astype(F32)
    send_rows = send.shape[0] // width
    total = jnp.zeros((rows, width), F32)
    for j in range(owner_ref.shape[0]):
        hot = (node_at == owner_ref[j : j + 1, :]).astype(F32).astype(BF16)
        source = send if j < send_rows else recv
        at = (j if j < send_rows else j - send_rows) * width
        total += mm(hot, source[at : at + width, :])
    nodes = nodes_ref[...]
    hidden = mm(nodes, w_in_ref[0:width, :]) + mm(total.astype(BF16), w_in_ref[width : 2 * width, :])
    hidden = jnp.maximum(hidden + bias_ref[0:1, :], 0.0).astype(BF16)
    hidden = jnp.maximum(mm(hidden, w_out_ref[0]) + bias_ref[1:2, :], 0.0).astype(BF16)
    output = mm(hidden, w_out_ref[1]) + bias_ref[2:3, :]
    mean = jnp.mean(output, axis=-1, keepdims=True)
    centred = output - mean
    spread = jnp.mean(centred * centred, axis=-1, keepdims=True)
    update = centred * lax.rsqrt(spread + 1e-05) * gain_ref[...] + shift_ref[...]
    out_ref[...] = (nodes.astype(F32) + update).astype(BF16)


def local(
    nodes,
    edges,
    send_list,
    recv_list,
    sender_slot,
    receiver_slot,
    tile_count,
    edge_in_weight,
    edge_out_weight,
    edge_bias,
    edge_gain,
    edge_shift,
    node_in_weight,
    node_out_weight,
    node_bias,
    node_gain,
    node_shift,
):
    rows, width = nodes.shape
    send_peers, send_depth = send_list.shape
    recv_peers, recv_depth = recv_list.shape
    chunk = rows + EXTRA
    params = pltpu.CompilerParams(vmem_limit_bytes=40 * 1024 * 1024)
    row_send, col_send = pl.pallas_call(
        pack_kernel,
        out_shape=(
            jax.ShapeDtypeStruct((recv_peers, chunk, width), BF16),
            jax.ShapeDtypeStruct((chunk, width), BF16),
        ),
        in_specs=[VMEM] * 3,
        out_specs=(VMEM, VMEM),
        compiler_params=params,
    )(nodes, send_list, recv_list)
    row_block = lax.all_to_all(row_send, "row", 0, 0, tiled=True)
    col_block = lax.all_gather(col_send, "col", axis=0, tiled=True).reshape(
        send_peers, chunk, width
    )
    place = lax.axis_index("col").astype(jnp.int32).reshape(1)
    new_edges, send_part, recv_part, owner = pl.pallas_call(
        edge_kernel,
        out_shape=(
            jax.ShapeDtypeStruct(edges.shape, BF16),
            jax.ShapeDtypeStruct((send_peers, send_depth, width), BF16),
            jax.ShapeDtypeStruct((recv_peers, recv_depth, width), BF16),
            jax.ShapeDtypeStruct((8, width), F32),
        ),
        in_specs=[SMEM, SMEM] + [VMEM] * 12,
        out_specs=(VMEM,) * 4,
        scratch_shapes=[
            pltpu.VMEM((send_peers * send_depth, width), F32),
            pltpu.VMEM((recv_peers * recv_depth, width), F32),
        ],
        compiler_params=params,
        cost_estimate=pl.CostEstimate(
            flops=2 * 10**9, bytes_accessed=4 * 10**6, transcendentals=4096
        ),
    )(
        tile_count,
        place,
        row_block,
        col_block,
        send_list,
        recv_list,
        sender_slot,
        receiver_slot,
        edges,
        edge_in_weight,
        edge_out_weight,
        edge_bias,
        edge_gain.reshape(1, width),
        edge_shift.reshape(1, width),
    )
    recv_in = lax.all_to_all(recv_part, "row", 0, 0, tiled=True)
    send_in = lax.all_to_all(send_part, "col", 0, 0, tiled=True)
    new_nodes = pl.pallas_call(
        node_kernel,
        out_shape=jax.ShapeDtypeStruct(nodes.shape, BF16),
        in_specs=[VMEM] * 9,
        out_specs=VMEM,
        compiler_params=params,
    )(
        owner,
        send_in,
        recv_in,
        nodes,
        node_in_weight,
        node_out_weight,
        node_bias,
        node_gain.reshape(1, width),
        node_shift.reshape(1, width),
    )
    return (new_nodes, new_edges)


def solution(mesh):
    split = P(("row", "col"), None)
    placed = (split,) * 6 + (P(("row", "col")),) + (P(),) * 10
    return jax.shard_map(
        local,
        mesh=mesh,
        in_specs=placed,
        out_specs=(split, split),
        check_vma=False,
    )
```

time: 399 us -> 97.2 us (0.24)
  waiting for transfers between devices: 326 us -> 0.01 us
  blocking collectives: 32.1 us -> 70.1 us
  between operations: 14.1 us -> 0.84 us
  Pallas kernels: 0 us -> 12 us
  other arithmetic: 12 us -> 0 us
  starting transfers between devices: 0.12 us -> 10.6 us
  local copies, waits for them, and re-layouts: 7.59 us -> 2.32 us
    reduce_scatter x2 -> x0, waiting for transfers between devices: 295 us -> none  [the longest x1 182 us: local(): lax.psum_scatter(send_full.astype(jnp.bfloat16), 'col', scatter_dimension...]
    all_to_all x0 -> x2, blocking collectives: none -> 39.1 us  [the longest x1 20.8 us: local(): recv_in = lax.all_to_all(recv_part, 'row', 0, 0, tiled=True)]
    all_gather x1 -> x0, waiting for transfers between devices: 30.2 us -> none  [local(): recv_block = lax.all_gather(nodes, 'row', axis=0, tiled=True)]
    pallas_call x0 -> x3, Pallas kernels: none -> 12 us  [the longest x1 9.35 us: local(): pl.pallas_call(edge_kernel, out_shape=(jax.ShapeDtypeStruct(edges.shape,...]
    all_to_all x0 -> x1, starting transfers between devices: none -> 10.6 us  [local(): row_block = lax.all_to_all(row_send, 'row', 0, 0, tiled=True)]
    scatter-add x2 -> x0, other arithmetic: 5.26 us -> none  [the longest x1 2.75 us: local(): jnp.zeros((recv_block.shape[0], width), jnp.float32).at[recv_pick]]
  transfers between devices with their start and end apart: 3 -> 1, of which waited for: 3 -> 0; matrix products, arithmetic and copies ran while one was open for 2% -> 0% of each run, Pallas kernels for 0% -> 0%
where the time goes in v1:
time: 97.2 us; the launch traced here: 95.8 us
  blocking collectives  70.1 us (72%)
  Pallas kernels  12 us (12%)
  starting transfers between devices  10.6 us (11%)
  local copies, waits for them, and re-layouts  2.32 us (2%)
    all_gather x1, blocking collectives, local(): lax.all_gather(col_send, 'col', axis=0, tiled=True)  31 us
    all_to_all x1, blocking collectives, local(): recv_in = lax.all_to_all(recv_part, 'row', 0, 0, tiled=True)  20.8 us
    all_to_all x1, blocking collectives, local(): send_in = lax.all_to_all(send_part, 'col', 0, 0, tiled=True)  18.2 us
    all_to_all x1, starting transfers between devices, local(): row_block = lax.all_to_all(row_send, 'row', 0, 0, tiled=True)  10.6 us
    pallas_call x1, Pallas kernels, local(): pl.pallas_call(edge_kernel, out_shape=(jax.ShapeDtypeStruct(edges.shape,...  9.35 us
    unnamed x37, local copies, waits for them, and re-layouts  2.32 us
  transfers between devices with their start and end apart: 1, of which 0 were waited for; matrix products, arithmetic and copies ran while one was open for 0% of the time, Pallas kernels for 0%

profile of v1, /device:TPU:1, one launch (start us, length us, event | category | flops | bytes accessed | tf_op | source)
XLA Modules:
  0.0 95.8 jit_solution(3578940976734028509)
XLA Ops:
  0.6 0.8 copy.19.recv_list_ref
  1.4 0.0 copy-start
  1.4 0.8 copy-done
  2.2 0.0 copy-start.4
  2.2 0.7 copy-done.4
  2.9 1.2 %shard_map.176 = (bf16[32,144,128]{2,1,0:T(8,128)(2,1)}, bf16[144,128]{1,0:T(8,128)(2,1)S(1)}) custom-call(bf16[128,128]{1,0:T(8,128)(2,1)S(1)} %copy-done, s32[16,32]{1,0:T(8,128)S(1)} %copy-done.4, s32[32,16]{1,0:T(8,128)S(1)} %copy.19.recv_list_ref), custom_call_target="tpu_custom_call" | custom-call | tf_op jit(solution)/shard_map/pallas_call | solution.py:233
  4.1 0.0 copy-start.5
  4.1 0.0 copy-start.9
  4.1 0.0 copy-start.10
  4.1 0.0 copy-start.11
  4.1 0.0 copy-start.12
  4.1 0.0 copy-start.13
  4.1 0.0 copy-start.14
  4.1 0.0 copy-start.15
  4.1 0.0 copy-start.16
  4.1 0.0 copy-start.17
  4.2 10.6 %all-to-all-start = ((bf16[32,144,128]{2,1,0:T(8,128)(2,1)}), bf16[32,144,128]{2,1,0:T(8,128)(2,1)S(1)}, u32[]{:S(2)}, u32[]{:S(2)}) async-start(bf16[32,144,128]{2,1,0:T(8,128)(2,1)} %get-tuple-element.8), calls=%async_computation | async-start | bytes 2359296 | tf_op jit(solution)/shard_map/all_to_all | solution.py:243
  14.8 31.0 %all_gather.3 = bf16[2304,128]{1,0:T(8,128)(2,1)S(1)} all-gather(bf16[144,128]{1,0:T(8,128)(2,1)S(1)} %get-tuple-element.9), channel_id=1, replica_groups=mesh['row'=32,'col'=16] {'col'}, dimensions={0}, use_global_device_ids=true | all-gather | bytes 626688 | tf_op jit(solution)/shard_map/all_gather | solution.py:244
  45.8 0.0 all-to-all-done.row_ref
  45.8 0.0 copy-done.5
  45.8 0.0 copy-done.9
  45.8 0.0 copy-done.10
  45.8 0.0 copy-done.11
  45.8 0.0 copy-done.12
  45.8 0.0 copy-done.13
  45.8 0.0 copy-done.14
  45.8 0.0 copy-done.15
  45.9 0.0 copy-done.16
  45.9 0.0 copy-done.17
  45.9 0.0 copy-start.1
  45.9 0.0 copy-start.2
  45.9 0.0 copy-start.3
  45.9 0.0 copy-start.6
  45.9 0.0 copy-start.7
  45.9 0.0 copy-start.8
  45.9 9.3 %shard_map.177 = (bf16[3072,128]{1,0:T(8,128)(2,1)}, bf16[16,32,128]{2,1,0:T(8,128)(2,1)S(1)}, bf16[32,16,128]{2,1,0:T(8,128)(2,1)S(1)}, f32[8,128]{1,0:T(8,128)S(1)}) custom-call(s32[24]{0:T(128)S(1)} %copy-done.15, s32[1]{0:T(128)} %bitcast.place_ref, bf16[32,144,128]{2,1,0:T(8,128)(2,1)S(1)} %all-to-all-done.row_ref, bf16[16,144,128]{2,1,0:T(8,128)(2,1)S(1)} %bitcast.6, ...), custom_call_target="tpu_custom_call" | custom-call | flops 2000000000 | bytes 4000000 | tf_op jit(solution)/shard_map/pallas_call | solution.py:248
  55.3 20.8 %all_to_all.15.recv_ref = bf16[32,16,128]{2,1,0:T(8,128)(2,1)S(1)} all-to-all(bf16[32,16,128]{2,1,0:T(8,128)(2,1)S(1)} %get-tuple-element.12), channel_id=1, replica_groups=mesh['row'=32,'col'=16] {'row'}, dimensions={0} | all-to-all | bytes 262144 | tf_op jit(solution)/shard_map/all_to_all | solution.py:282
  76.1 18.2 %all_to_all.16.send_ref = bf16[16,32,128]{2,1,0:T(8,128)(2,1)S(1)} all-to-all(bf16[16,32,128]{2,1,0:T(8,128)(2,1)S(1)} %get-tuple-element.11), channel_id=1, replica_groups=mesh['row'=32,'col'=16] {'col'}, dimensions={0} | all-to-all | bytes 262144 | tf_op jit(solution)/shard_map/all_to_all | solution.py:283
  94.4 0.0 copy-done.1
  94.4 0.0 copy-done.2
  94.4 0.0 copy-done.3
  94.4 0.0 copy-done.6
  94.4 0.0 copy-done.7
  94.4 0.0 copy-done.8
  94.4 1.4 %shard_map.178 = bf16[128,128]{1,0:T(8,128)(2,1)} custom-call(f32[8,128]{1,0:T(8,128)S(1)} %get-tuple-element.10.owner_ref, bf16[16,32,128]{2,1,0:T(8,128)(2,1)S(1)} %all_to_all.16.send_ref, bf16[32,16,128]{2,1,0:T(8,128)(2,1)S(1)} %all_to_all.15.recv_ref, bf16[128,128]{1,0:T(8,128)(2,1)S(1)} %copy-done.1, bf16[256,128]{1,0:T(8,128)(2,1)S(1)} %copy-done.2, ...), custom_call_target="tpu_custom_call" | custom-call | tf_op jit(solution)/shard_map/pallas_call | solution.py:284
Async XLA Ops:
  1.4 0.8 copy-start
  2.2 0.7 copy-start.4
  4.1 41.7 %copy-start.5 = (s32[16,32]{1,0:T(8,128)S(1)}, s32[16,32]{1,0:T(8,128)}, u32[]{:S(2)}) copy-start(s32[16,32]{1,0:T(8,128)} %send_list_ref.3) | copy-start | bytes 6148
  4.1 41.7 %copy-start.9 = (bf16[3072,128]{1,0:T(8,128)(2,1)S(1)}, bf16[3072,128]{1,0:T(8,128)(2,1)}, u32[]{:S(2)}) copy-start(bf16[3072,128]{1,0:T(8,128)(2,1)} %edges_ref.1) | copy-start | bytes 2359300
  4.1 41.7 %copy-start.10 = (bf16[384,128]{1,0:T(8,128)(2,1)S(1)}, bf16[384,128]{1,0:T(8,128)(2,1)}, u32[]{:S(2)}) copy-start(bf16[384,128]{1,0:T(8,128)(2,1)} %w_in_ref.2) | copy-start | bytes 294916
  4.1 41.7 %copy-start.11 = (bf16[2,128,128]{2,1,0:T(8,128)(2,1)S(1)}, bf16[2,128,128]{2,1,0:T(8,128)(2,1)}, u32[]{:S(2)}) copy-start(bf16[2,128,128]{2,1,0:T(8,128)(2,1)} %w_out_ref.2) | copy-start | bytes 196612
  4.1 41.7 %copy-start.12 = (s32[24,128]{1,0:T(8,128)S(1)}, s32[24,128]{1,0:T(8,128)}, u32[]{:S(2)}) copy-start(s32[24,128]{1,0:T(8,128)} %send_slot_ref.1) | copy-start | bytes 36868
  4.1 41.7 %copy-start.13 = (s32[24,128]{1,0:T(8,128)S(1)}, s32[24,128]{1,0:T(8,128)}, u32[]{:S(2)}) copy-start(s32[24,128]{1,0:T(8,128)} %recv_slot_ref.1) | copy-start | bytes 36868
  4.1 41.7 %copy-start.14 = (f32[3,128]{1,0:T(4,128)S(1)}, f32[3,128]{1,0:T(4,128)}, u32[]{:S(2)}) copy-start(f32[3,128]{1,0:T(4,128)} %bias_ref.2) | copy-start | bytes 4612
  4.1 41.7 %copy-start.15 = (s32[24]{0:T(128)S(1)}, s32[24]{0:T(128)}, u32[]{:S(2)}) copy-start(s32[24]{0:T(128)} %count_ref.1) | copy-start | bytes 292
  4.1 41.7 %copy-start.16 = (f32[128]{0:T(128)S(1)}, f32[128]{0:T(128)}, u32[]{:S(2)}) copy-start(f32[128]{0:T(128)} %param.27) | copy-start | bytes 1540
  4.1 41.7 %copy-start.17 = (f32[128]{0:T(128)S(1)}, f32[128]{0:T(128)}, u32[]{:S(2)}) copy-start(f32[128]{0:T(128)} %param.28) | copy-start | bytes 1540
  4.2 41.6 %all-to-all-start = ((bf16[32,144,128]{2,1,0:T(8,128)(2,1)}), bf16[32,144,128]{2,1,0:T(8,128)(2,1)S(1)}, u32[]{:S(2)}, u32[]{:S(2)}) async-start(bf16[32,144,128]{2,1,0:T(8,128)(2,1)} %get-tuple-element.8), calls=%async_computation | async-start | bytes 2359296 | tf_op jit(solution)/shard_map/all_to_all | solution.py:243
  45.9 48.5 %copy-start.1 = (bf16[128,128]{1,0:T(8,128)(2,1)S(1)}, bf16[128,128]{1,0:T(8,128)(2,1)}, u32[]{:S(2)}) copy-start(bf16[128,128]{1,0:T(8,128)(2,1)} %nodes_ref.3) | copy-start | bytes 98308
  45.9 48.5 %copy-start.2 = (bf16[256,128]{1,0:T(8,128)(2,1)S(1)}, bf16[256,128]{1,0:T(8,128)(2,1)}, u32[]{:S(2)}) copy-start(bf16[256,128]{1,0:T(8,128)(2,1)} %w_in_ref.3) | copy-start | bytes 196612
  45.9 48.5 %copy-start.3 = (bf16[2,128,128]{2,1,0:T(8,128)(2,1)S(1)}, bf16[2,128,128]{2,1,0:T(8,128)(2,1)}, u32[]{:S(2)}) copy-start(bf16[2,128,128]{2,1,0:T(8,128)(2,1)} %w_out_ref.3) | copy-start | bytes 196612
  45.9 48.5 %copy-start.6 = (f32[3,128]{1,0:T(4,128)S(1)}, f32[3,128]{1,0:T(4,128)}, u32[]{:S(2)}) copy-start(f32[3,128]{1,0:T(4,128)} %bias_ref.3) | copy-start | bytes 4612
  45.9 48.5 %copy-start.7 = (f32[128]{0:T(128)S(1)}, f32[128]{0:T(128)}, u32[]{:S(2)}) copy-start(f32[128]{0:T(128)} %param.32) | copy-start | bytes 1540
  45.9 48.5 %copy-start.8 = (f32[128]{0:T(128)S(1)}, f32[128]{0:T(128)}, u32[]{:S(2)}) copy-start(f32[128]{0:T(128)} %param.33) | copy-start | bytes 1540

commit v2 on v1

--- a/solution.py
+++ b/solution.py
@@ -7,6 +7,7 @@
 
 F32 = jnp.float32
 BF16 = jnp.bfloat16
+I16 = jnp.int16
 EXTRA = 16
 VMEM = pl.BlockSpec(memory_space=pltpu.VMEM)
 SMEM = pl.BlockSpec(memory_space=pltpu.SMEM)
@@ -19,21 +20,25 @@
     return lax.dot_general(a, b, dims, preferred_element_type=F32)
 
 
-def repeat_lanes(lists, width):
-    depth = lists.shape[1]
+def repeat_lanes(lists, width, across):
+    depth = lists.shape[across]
     place = (
         lax.broadcasted_iota(jnp.int32, (depth, width), 1) % depth
         == lax.broadcasted_iota(jnp.int32, (depth, width), 0)
     )
-    return mm(lists.astype(F32).astype(BF16), place.astype(F32).astype(BF16))
+    return mm(
+        lists.astype(F32).astype(BF16),
+        place.astype(F32).astype(BF16),
+        (((across,), (0,)), ((), ())),
+    )
 
 
 def pack_kernel(nodes_ref, send_list_ref, recv_list_ref, row_ref, col_ref):
     rows, width = nodes_ref.shape
-    peers = recv_list_ref.shape[0]
+    peers = recv_list_ref.shape[1]
     col_ref[0:rows, :] = nodes_ref[...]
-    col_ref[rows : rows + EXTRA, :] = repeat_lanes(send_list_ref[...], width).astype(BF16)
-    recv_lanes = repeat_lanes(recv_list_ref[...], width)
+    col_ref[rows : rows + EXTRA, :] = repeat_lanes(send_list_ref[...], width, 1).astype(BF16)
+    recv_lanes = repeat_lanes(recv_list_ref[...], width, 0)
     for peer in range(peers):
         row_ref[peer, 0:rows, :] = nodes_ref[...]
         row_ref[peer, rows : rows + EXTRA, :] = jnp.broadcast_to(
@@ -72,19 +77,15 @@
     send_out_ref,
     recv_out_ref,
     owner_ref,
-    send_acc,
-    recv_acc,
 ):
     recv_peers, chunk, width = row_ref.shape
     send_peers = col_ref.shape[0]
     rows = chunk - EXTRA
     send_depth = send_list_ref.shape[1]
-    recv_depth = recv_list_ref.shape[1]
+    recv_depth = recv_list_ref.shape[0]
     send_width = send_peers * send_depth
     recv_width = recv_peers * recv_depth
     tiles, tile = send_slot_ref.shape
-    group = 4
-    step_rows = group * tile
 
     me = place_ref[0]
     mine = lax.broadcasted_iota(jnp.int32, (EXTRA, width), 0) == me
@@ -104,16 +105,18 @@
     owner_ref[...] = jnp.concatenate(send_owner + recv_owner, axis=0)
 
     node_at = lax.broadcasted_iota(jnp.int32, (rows, 1), 0)
-
-    def table(block_ref, list_ref, peers):
-        parts = []
-        for p in range(peers):
-            hot = (node_at == list_ref[p : p + 1, :]).astype(F32).astype(BF16)
-            parts.append(mm(hot, block_ref[p, 0:rows, :], TN))
-        return jnp.concatenate(parts, axis=0).astype(BF16)
-
-    send_table = table(col_ref, send_list_ref, send_peers)
-    recv_table = table(row_ref, recv_list_ref, recv_peers)
+    node_lane = lax.broadcasted_iota(jnp.int32, (1, rows), 1)
+    parts = []
+    for p in range(send_peers):
+        hot = (node_at == send_list_ref[p : p + 1, :]).astype(F32).astype(BF16)
+        parts.append(mm(hot, col_ref[p, 0:rows, :], TN))
+    send_table = jnp.concatenate(parts, axis=0).astype(BF16)
+    parts = []
+    recv_list = recv_list_ref[...]
+    for p in range(recv_peers):
+        hot = (recv_list[:, p : p + 1] == node_lane).astype(F32).astype(BF16)
+        parts.append(mm(hot, row_ref[p, 0:rows, :]))
+    recv_table = jnp.concatenate(parts, axis=0).astype(BF16)
     send_proj = mm(send_table, w_in_ref[width : 2 * width, :]).T.astype(BF16)
     recv_proj = mm(recv_table, w_in_ref[2 * width : 3 * width, :]).T.astype(BF16)
     edge_w = w_in_ref[0:width, :].astype(F32).T.astype(BF16)
@@ -125,50 +128,33 @@
     b0, b1, b2 = columns[:, 0:1], columns[:, 1:2], columns[:, 2:3]
     gain, shift = columns[:, 3:4], columns[:, 4:5]
 
-    send_at = lax.broadcasted_iota(jnp.int32, (send_width, tile), 0)
-    recv_at = lax.broadcasted_iota(jnp.int32, (recv_width, tile), 0)
-    row_at = lax.broadcasted_iota(jnp.int32, (tile, 1), 0)
-
-    for step in range(tiles // group):
-        first = step * group
-        send_hot = jnp.concatenate(
+    def one_hot(slot_ref, entries):
+        at = lax.broadcasted_iota(jnp.int32, (entries, tile), 0).astype(I16)
+        return jnp.concatenate(
             [
-                (send_at == send_slot_ref[first + t : first + t + 1, :]).astype(F32).astype(BF16)
-                for t in range(group)
+                jnp.where(at == slot_ref[t : t + 1, :].astype(I16), BF16(1), BF16(0))
+                for t in range(tiles)
             ],
             axis=1,
         )
-        recv_hot = jnp.concatenate(
-            [
-                (recv_at == recv_slot_ref[first + t : first + t + 1, :]).astype(F32).astype(BF16)
-                for t in range(group)
-            ],
-            axis=1,
-        )
-        edge = edges_ref[first * tile : first * tile + step_rows, :]
-        hidden = mm(send_proj, send_hot) + mm(recv_proj, recv_hot) + mm(edge_w, edge, NT)
-        hidden = jnp.maximum(hidden + b0, 0.0).astype(BF16)
-        hidden = jnp.maximum(mm(mid_w, hidden) + b1, 0.0).astype(BF16)
-        output = mm(last_w, hidden) + b2
-        mean = jnp.sum(output, axis=0, keepdims=True) * (1.0 / width)
-        centred = output - mean
-        spread = jnp.sum(centred * centred, axis=0, keepdims=True) * (1.0 / width)
-        update = (centred * lax.rsqrt(spread + 1e-05) * gain + shift).T
-        valid = jnp.concatenate(
-            [row_at < count_ref[first + t] for t in range(group)], axis=0
-        )
-        fresh = jnp.where(valid, edge.astype(F32) + update, 0.0).astype(BF16)
-        new_ref[first * tile : first * tile + step_rows, :] = fresh
-        send_sum = mm(send_hot, fresh)
-        recv_sum = mm(recv_hot, fresh)
-        if step == 0:
-            send_acc[...] = send_sum
-            recv_acc[...] = recv_sum
-        else:
-            send_acc[...] += send_sum
-            recv_acc[...] += recv_sum
-    send_out_ref[...] = send_acc[...].astype(BF16).reshape(send_out_ref.shape)
-    recv_out_ref[...] = recv_acc[...].astype(BF16).reshape(recv_out_ref.shape)
+
+    send_hot = one_hot(send_slot_ref, send_width)
+    recv_hot = one_hot(recv_slot_ref, recv_width)
+    edge = edges_ref[...]
+    hidden = mm(send_proj, send_hot) + mm(recv_proj, recv_hot) + mm(edge_w, edge, NT)
+    hidden = jnp.maximum(hidden + b0, 0.0).astype(BF16)
+    hidden = jnp.maximum(mm(mid_w, hidden) + b1, 0.0).astype(BF16)
+    output = mm(last_w, hidden) + b2
+    mean = jnp.sum(output, axis=0, keepdims=True) * (1.0 / width)
+    centred = output - mean
+    spread = jnp.sum(centred * centred, axis=0, keepdims=True) * (1.0 / width)
+    update = (centred * lax.rsqrt(spread + 1e-05) * gain + shift).T
+    row_at = lax.broadcasted_iota(jnp.int32, (tile, 1), 0)
+    valid = jnp.concatenate([row_at < count_ref[t] for t in range(tiles)], axis=0)
+    fresh = jnp.where(valid, edge.astype(F32) + update, 0.0).astype(BF16)
+    new_ref[...] = fresh
+    send_out_ref[...] = mm(send_hot, fresh).astype(BF16).reshape(send_out_ref.shape)
+    recv_out_ref[...] = mm(recv_hot, fresh).astype(BF16).reshape(recv_out_ref.shape)
 
 
 def node_kernel(
@@ -227,7 +213,8 @@
 ):
     rows, width = nodes.shape
     send_peers, send_depth = send_list.shape
-    recv_peers, recv_depth = recv_list.shape
+    recv_list = recv_list.T
+    recv_depth, recv_peers = recv_list.shape
     chunk = rows + EXTRA
     params = pltpu.CompilerParams(vmem_limit_bytes=40 * 1024 * 1024)
     row_send, col_send = pl.pallas_call(
@@ -238,7 +225,7 @@
         ),
         in_specs=[VMEM] * 3,
         out_specs=(VMEM, VMEM),
-        compiler_params=params,
+        compiler_params=pltpu.CompilerParams(vmem_limit_bytes=60 * 1024 * 1024),
     )(nodes, send_list, recv_list)
     row_block = lax.all_to_all(row_send, "row", 0, 0, tiled=True)
     col_block = lax.all_gather(col_send, "col", axis=0, tiled=True).reshape(
@@ -255,10 +242,6 @@
         ),
         in_specs=[SMEM, SMEM] + [VMEM] * 12,
         out_specs=(VMEM,) * 4,
-        scratch_shapes=[
-            pltpu.VMEM((send_peers * send_depth, width), F32),
-            pltpu.VMEM((recv_peers * recv_depth, width), F32),
-        ],
         compiler_params=params,
         cost_estimate=pl.CostEstimate(
             flops=2 * 10**9, bytes_accessed=4 * 10**6, transcendentals=4096

time: 97.2 us -> 91.4 us (0.940)
  Pallas kernels: 12 us -> 8.39 us
  local copies, waits for them, and re-layouts: 2.32 us -> 0.11 us
    pallas_call x1, Pallas kernels: 9.35 us -> 4.98 us  [local(): pl.pallas_call(edge_kernel, out_shape=(jax.ShapeDtypeStruct(edges.shape,...]
    unnamed x37 -> x36, local copies, waits for them, and re-layouts: 2.32 us -> 0.11 us
where the time goes in v2:
time: 91.4 us; the launch traced here: 90.1 us
  blocking collectives  70.1 us (77%)
  starting transfers between devices  10.6 us (12%)
  Pallas kernels  8.39 us (9%)
    all_gather x1, blocking collectives, local(): lax.all_gather(col_send, 'col', axis=0, tiled=True)  31 us
    all_to_all x1, blocking collectives, local(): recv_in = lax.all_to_all(recv_part, 'row', 0, 0, tiled=True)  20.8 us
    all_to_all x1, blocking collectives, local(): send_in = lax.all_to_all(send_part, 'col', 0, 0, tiled=True)  18.2 us
    all_to_all x1, starting transfers between devices, local(): row_block = lax.all_to_all(row_send, 'row', 0, 0, tiled=True)  10.6 us
    pallas_call x1, Pallas kernels, local(): pl.pallas_call(edge_kernel, out_shape=(jax.ShapeDtypeStruct(edges.shape,...  4.98 us
    pallas_call x1, Pallas kernels, local(): pl.pallas_call(pack_kernel, out_shape=(jax.ShapeDtypeStruct((recv_peers,...  2 us
  transfers between devices with their start and end apart: 1, of which 0 were waited for; matrix products, arithmetic and copies ran while one was open for 0% of the time, Pallas kernels for 0%

profile of v2, /device:TPU:1, one launch (start us, length us, event | category | flops | bytes accessed | tf_op | source)
XLA Modules:
  0.0 90.1 jit_solution(4174899307292977255)
XLA Ops:
  0.6 2.0 %shard_map.176 = (bf16[32,144,128]{2,1,0:T(8,128)(2,1)}, bf16[144,128]{1,0:T(8,128)(2,1)}) custom-call(bf16[128,128]{1,0:T(8,128)(2,1)} %nodes_ref.3, s32[16,32]{1,0:T(8,128)} %send_list_ref.3, s32[16,32]{1,0:T(8,128)} %bitcast.8), custom_call_target="tpu_custom_call" | custom-call | tf_op jit(solution)/shard_map/pallas_call | solution.py:220
  2.6 0.0 copy-start.17
  2.6 0.0 copy-start.3
  2.6 0.0 copy-start.4
  2.6 0.0 copy-start.8
  2.7 0.0 copy-start.9
  2.7 0.0 copy-start.10
  2.7 0.0 copy-start.11
  2.7 0.0 copy-start.12
  2.7 0.0 copy-start.13
  2.7 0.0 copy-start.14
  2.7 0.0 copy-start.15
  2.7 0.0 copy-start.16
  2.8 10.6 %all-to-all-start = ((bf16[32,144,128]{2,1,0:T(8,128)(2,1)}), bf16[32,144,128]{2,1,0:T(8,128)(2,1)S(1)}, u32[]{:S(2)}, u32[]{:S(2)}) async-start(bf16[32,144,128]{2,1,0:T(8,128)(2,1)} %get-tuple-element.8), calls=%async_computation | async-start | bytes 2359296 | tf_op jit(solution)/shard_map/all_to_all | solution.py:230
  13.4 0.0 copy-done.17
  13.4 31.0 %all_gather.3 = bf16[2304,128]{1,0:T(8,128)(2,1)S(1)} all-gather(bf16[144,128]{1,0:T(8,128)(2,1)S(1)} %copy-done.17), channel_id=1, replica_groups=mesh['row'=32,'col'=16] {'col'}, dimensions={0}, use_global_device_ids=true | all-gather | bytes 626688 | tf_op jit(solution)/shard_map/all_gather | solution.py:231
  44.4 0.0 all-to-all-done.row_ref
  44.4 0.0 copy-done.3
  44.4 0.0 copy-done.4
  44.4 0.0 copy-done.8
  44.4 0.0 copy-done.9
  44.4 0.0 copy-done.10
  44.4 0.0 copy-done.11
  44.4 0.0 copy-done.12
  44.4 0.0 copy-done.13
  44.5 0.0 copy-done.14
  44.5 0.0 copy-done.15
  44.5 0.0 copy-done.16
  44.5 0.0 copy-start
  44.5 0.0 copy-start.1
  44.5 0.0 copy-start.2
  44.5 0.0 copy-start.5
  44.5 0.0 copy-start.6
  44.5 0.0 copy-start.7
  44.6 5.0 %shard_map.177 = (bf16[3072,128]{1,0:T(8,128)(2,1)}, bf16[16,32,128]{2,1,0:T(8,128)(2,1)S(1)}, bf16[32,16,128]{2,1,0:T(8,128)(2,1)S(1)}, f32[8,128]{1,0:T(8,128)S(1)}) custom-call(s32[24]{0:T(128)S(1)} %copy-done.14, s32[1]{0:T(128)} %bitcast.place_ref, bf16[32,144,128]{2,1,0:T(8,128)(2,1)S(1)} %all-to-all-done.row_ref, bf16[16,144,128]{2,1,0:T(8,128)(2,1)S(1)} %bitcast.7, ...), custom_call_target="tpu_custom_call" | custom-call | flops 2000000000 | bytes 4000000 | tf_op jit(solution)/shard_map/pallas_call | solution.py:235
  49.5 20.8 %all_to_all.15.recv_ref = bf16[32,16,128]{2,1,0:T(8,128)(2,1)S(1)} all-to-all(bf16[32,16,128]{2,1,0:T(8,128)(2,1)S(1)} %get-tuple-element.12), channel_id=1, replica_groups=mesh['row'=32,'col'=16] {'row'}, dimensions={0} | all-to-all | bytes 262144 | tf_op jit(solution)/shard_map/all_to_all | solution.py:265
  70.4 18.2 %all_to_all.16.send_ref = bf16[16,32,128]{2,1,0:T(8,128)(2,1)S(1)} all-to-all(bf16[16,32,128]{2,1,0:T(8,128)(2,1)S(1)} %get-tuple-element.11), channel_id=1, replica_groups=mesh['row'=32,'col'=16] {'col'}, dimensions={0} | all-to-all | bytes 262144 | tf_op jit(solution)/shard_map/all_to_all | solution.py:266
  88.6 0.0 copy-done
  88.6 0.0 copy-done.1
  88.6 0.0 copy-done.2
  88.6 0.0 copy-done.5
  88.6 0.0 copy-done.6
  88.7 0.0 copy-done.7
  88.7 1.4 %shard_map.178 = bf16[128,128]{1,0:T(8,128)(2,1)} custom-call(f32[8,128]{1,0:T(8,128)S(1)} %get-tuple-element.10.owner_ref, bf16[16,32,128]{2,1,0:T(8,128)(2,1)S(1)} %all_to_all.16.send_ref, bf16[32,16,128]{2,1,0:T(8,128)(2,1)S(1)} %all_to_all.15.recv_ref, bf16[128,128]{1,0:T(8,128)(2,1)S(1)} %copy-done, bf16[256,128]{1,0:T(8,128)(2,1)S(1)} %copy-done.1, ...), custom_call_target="tpu_custom_call" | custom-call | tf_op jit(solution)/shard_map/pallas_call | solution.py:267
Async XLA Ops:
  2.6 10.7 %copy-start.17 = (bf16[144,128]{1,0:T(8,128)(2,1)S(1)}, bf16[144,128]{1,0:T(8,128)(2,1)}, u32[]{:S(2)}) copy-start(bf16[144,128]{1,0:T(8,128)(2,1)} %get-tuple-element.9) | copy-start | bytes 110596
  2.6 41.8 %copy-start.3 = (s32[16,32]{1,0:T(8,128)S(1)}, s32[16,32]{1,0:T(8,128)}, u32[]{:S(2)}) copy-start(s32[16,32]{1,0:T(8,128)} %send_list_ref.3) | copy-start | bytes 6148
  2.6 41.8 %copy-start.4 = (s32[32,16]{0,1:T(8,128)S(1)}, s32[32,16]{0,1:T(8,128)}, u32[]{:S(2)}) copy-start(s32[32,16]{0,1:T(8,128)} %param.20) | copy-start | bytes 6148
  2.6 41.8 %copy-start.8 = (bf16[3072,128]{1,0:T(8,128)(2,1)S(1)}, bf16[3072,128]{1,0:T(8,128)(2,1)}, u32[]{:S(2)}) copy-start(bf16[3072,128]{1,0:T(8,128)(2,1)} %edges_ref.1) | copy-start | bytes 2359300
  2.7 41.8 %copy-start.9 = (bf16[384,128]{1,0:T(8,128)(2,1)S(1)}, bf16[384,128]{1,0:T(8,128)(2,1)}, u32[]{:S(2)}) copy-start(bf16[384,128]{1,0:T(8,128)(2,1)} %w_in_ref.2) | copy-start | bytes 294916
  2.7 41.8 %copy-start.10 = (bf16[2,128,128]{2,1,0:T(8,128)(2,1)S(1)}, bf16[2,128,128]{2,1,0:T(8,128)(2,1)}, u32[]{:S(2)}) copy-start(bf16[2,128,128]{2,1,0:T(8,128)(2,1)} %w_out_ref.2) | copy-start | bytes 196612
  2.7 41.7 %copy-start.11 = (s32[24,128]{1,0:T(8,128)S(1)}, s32[24,128]{1,0:T(8,128)}, u32[]{:S(2)}) copy-start(s32[24,128]{1,0:T(8,128)} %send_slot_ref.1) | copy-start | bytes 36868
  2.7 41.7 %copy-start.12 = (s32[24,128]{1,0:T(8,128)S(1)}, s32[24,128]{1,0:T(8,128)}, u32[]{:S(2)}) copy-start(s32[24,128]{1,0:T(8,128)} %recv_slot_ref.1) | copy-start | bytes 36868
  2.7 41.7 %copy-start.13 = (f32[3,128]{1,0:T(4,128)S(1)}, f32[3,128]{1,0:T(4,128)}, u32[]{:S(2)}) copy-start(f32[3,128]{1,0:T(4,128)} %bias_ref.2) | copy-start | bytes 4612
  2.7 41.7 %copy-start.14 = (s32[24]{0:T(128)S(1)}, s32[24]{0:T(128)}, u32[]{:S(2)}) copy-start(s32[24]{0:T(128)} %count_ref.1) | copy-start | bytes 292
  2.7 41.7 %copy-start.15 = (f32[128]{0:T(128)S(1)}, f32[128]{0:T(128)}, u32[]{:S(2)}) copy-start(f32[128]{0:T(128)} %param.27) | copy-start | bytes 1540
  2.7 41.7 %copy-start.16 = (f32[128]{0:T(128)S(1)}, f32[128]{0:T(128)}, u32[]{:S(2)}) copy-start(f32[128]{0:T(128)} %param.28) | copy-start | bytes 1540
  2.8 41.6 %all-to-all-start = ((bf16[32,144,128]{2,1,0:T(8,128)(2,1)}), bf16[32,144,128]{2,1,0:T(8,128)(2,1)S(1)}, u32[]{:S(2)}, u32[]{:S(2)}) async-start(bf16[32,144,128]{2,1,0:T(8,128)(2,1)} %get-tuple-element.8), calls=%async_computation | async-start | bytes 2359296 | tf_op jit(solution)/shard_map/all_to_all | solution.py:230
  44.5 44.1 %copy-start = (bf16[128,128]{1,0:T(8,128)(2,1)S(1)}, bf16[128,128]{1,0:T(8,128)(2,1)}, u32[]{:S(2)}) copy-start(bf16[128,128]{1,0:T(8,128)(2,1)} %nodes_ref.3) | copy-start | bytes 98308
  44.5 44.1 %copy-start.1 = (bf16[256,128]{1,0:T(8,128)(2,1)S(1)}, bf16[256,128]{1,0:T(8,128)(2,1)}, u32[]{:S(2)}) copy-start(bf16[256,128]{1,0:T(8,128)(2,1)} %w_in_ref.3) | copy-start | bytes 196612
  44.5 44.1 %copy-start.2 = (bf16[2,128,128]{2,1,0:T(8,128)(2,1)S(1)}, bf16[2,128,128]{2,1,0:T(8,128)(2,1)}, u32[]{:S(2)}) copy-start(bf16[2,128,128]{2,1,0:T(8,128)(2,1)} %w_out_ref.3) | copy-start | bytes 196612
  44.5 44.1 %copy-start.5 = (f32[3,128]{1,0:T(4,128)S(1)}, f32[3,128]{1,0:T(4,128)}, u32[]{:S(2)}) copy-start(f32[3,128]{1,0:T(4,128)} %bias_ref.3) | copy-start | bytes 4612
  44.5 44.1 %copy-start.6 = (f32[128]{0:T(128)S(1)}, f32[128]{0:T(128)}, u32[]{:S(2)}) copy-start(f32[128]{0:T(128)} %param.32) | copy-start | bytes 1540
  44.5 44.1 %copy-start.7 = (f32[128]{0:T(128)S(1)}, f32[128]{0:T(128)}, u32[]{:S(2)}) copy-start(f32[128]{0:T(128)} %param.33) | copy-start | bytes 1540

commit v3 on v2

--- a/solution.py
+++ b/solution.py
@@ -77,6 +77,8 @@
     send_out_ref,
     recv_out_ref,
     owner_ref,
+    new_vmem,
+    sem,
 ):
     recv_peers, chunk, width = row_ref.shape
     send_peers = col_ref.shape[0]
@@ -138,10 +140,12 @@
             axis=1,
         )
 
-    send_hot = one_hot(send_slot_ref, send_width)
-    recv_hot = one_hot(recv_slot_ref, recv_width)
+    hot = jnp.concatenate(
+        [one_hot(send_slot_ref, send_width), one_hot(recv_slot_ref, recv_width)], axis=0
+    )
+    proj = jnp.concatenate([send_proj, recv_proj], axis=1)
     edge = edges_ref[...]
-    hidden = mm(send_proj, send_hot) + mm(recv_proj, recv_hot) + mm(edge_w, edge, NT)
+    hidden = mm(proj, hot) + mm(edge_w, edge, NT)
     hidden = jnp.maximum(hidden + b0, 0.0).astype(BF16)
     hidden = jnp.maximum(mm(mid_w, hidden) + b1, 0.0).astype(BF16)
     output = mm(last_w, hidden) + b2
@@ -152,9 +156,13 @@
     row_at = lax.broadcasted_iota(jnp.int32, (tile, 1), 0)
     valid = jnp.concatenate([row_at < count_ref[t] for t in range(tiles)], axis=0)
     fresh = jnp.where(valid, edge.astype(F32) + update, 0.0).astype(BF16)
-    new_ref[...] = fresh
-    send_out_ref[...] = mm(send_hot, fresh).astype(BF16).reshape(send_out_ref.shape)
-    recv_out_ref[...] = mm(recv_hot, fresh).astype(BF16).reshape(recv_out_ref.shape)
+    new_vmem[...] = fresh
+    copy = pltpu.make_async_copy(new_vmem, new_ref, sem)
+    copy.start()
+    sums = mm(hot, fresh).astype(BF16)
+    send_out_ref[...] = sums[0:send_width, :].reshape(send_out_ref.shape)
+    recv_out_ref[...] = sums[send_width:, :].reshape(recv_out_ref.shape)
+    copy.wait()
 
 
 def node_kernel(
@@ -170,16 +178,18 @@
     out_ref,
 ):
     rows, width = nodes_ref.shape
-    send = send_ref[...].reshape(-1, width)
-    recv = recv_ref[...].reshape(-1, width)
+    partial = jnp.concatenate(
+        [send_ref[...].reshape(-1, width), recv_ref[...].reshape(-1, width)], axis=0
+    )
     node_at = lax.broadcasted_iota(jnp.int32, (rows, width), 0).astype(F32)
-    send_rows = send.shape[0] // width
-    total = jnp.zeros((rows, width), F32)
-    for j in range(owner_ref.shape[0]):
-        hot = (node_at == owner_ref[j : j + 1, :]).astype(F32).astype(BF16)
-        source = send if j < send_rows else recv
-        at = (j if j < send_rows else j - send_rows) * width
-        total += mm(hot, source[at : at + width, :])
+    hot = jnp.concatenate(
+        [
+            (node_at == owner_ref[j : j + 1, :]).astype(F32).astype(BF16)
+            for j in range(owner_ref.shape[0])
+        ],
+        axis=1,
+    )
+    total = mm(hot, partial)
     nodes = nodes_ref[...]
     hidden = mm(nodes, w_in_ref[0:width, :]) + mm(total.astype(BF16), w_in_ref[width : 2 * width, :])
     hidden = jnp.maximum(hidden + bias_ref[0:1, :], 0.0).astype(BF16)
@@ -241,7 +251,8 @@
             jax.ShapeDtypeStruct((8, width), F32),
         ),
         in_specs=[SMEM, SMEM] + [VMEM] * 12,
-        out_specs=(VMEM,) * 4,
+        out_specs=(pl.BlockSpec(memory_space=pl.ANY), VMEM, VMEM, VMEM),
+        scratch_shapes=[pltpu.VMEM(edges.shape, BF16), pltpu.SemaphoreType.DMA(())],
         compiler_params=params,
         cost_estimate=pl.CostEstimate(
             flops=2 * 10**9, bytes_accessed=4 * 10**6, transcendentals=4096

time: 91.4 us -> 91.1 us (level)
  no operation moved by 1% of the time
where the time goes in v3:
time: 91.1 us; the launch traced here: 89.8 us
  blocking collectives  70.1 us (77%)
  starting transfers between devices  10.6 us (12%)
  Pallas kernels  8.08 us (9%)
    all_gather x1, blocking collectives, local(): lax.all_gather(col_send, 'col', axis=0, tiled=True)  31 us
    all_to_all x1, blocking collectives, local(): recv_in = lax.all_to_all(recv_part, 'row', 0, 0, tiled=True)  20.9 us
    all_to_all x1, blocking collectives, local(): send_in = lax.all_to_all(send_part, 'col', 0, 0, tiled=True)  18.3 us
    all_to_all x1, starting transfers between devices, local(): row_block = lax.all_to_all(row_send, 'row', 0, 0, tiled=True)  10.6 us
    pallas_call x1, Pallas kernels, local(): pl.pallas_call(edge_kernel, out_shape=(jax.ShapeDtypeStruct(edges.shape,...  4.7 us
    pallas_call x1, Pallas kernels, local(): pl.pallas_call(pack_kernel, out_shape=(jax.ShapeDtypeStruct((recv_peers,...  2 us
  transfers between devices with their start and end apart: 1, of which 0 were waited for; matrix products, arithmetic and copies ran while one was open for 0% of the time, Pallas kernels for 0%

profile of v3, /device:TPU:1, one launch (start us, length us, event | category | flops | bytes accessed | tf_op | source)
XLA Modules:
  0.0 89.8 jit_solution(1390256810824658007)
XLA Ops:
  0.6 2.0 %shard_map.176 = (bf16[32,144,128]{2,1,0:T(8,128)(2,1)}, bf16[144,128]{1,0:T(8,128)(2,1)}) custom-call(bf16[128,128]{1,0:T(8,128)(2,1)} %nodes_ref.3, s32[16,32]{1,0:T(8,128)} %send_list_ref.3, s32[16,32]{1,0:T(8,128)} %bitcast.8), custom_call_target="tpu_custom_call" | custom-call | tf_op jit(solution)/shard_map/pallas_call | solution.py:230
  2.6 0.0 copy-start.17
  2.6 0.0 copy-start.3
  2.6 0.0 copy-start.4
  2.6 0.0 copy-start.8
  2.7 0.0 copy-start.9
  2.7 0.0 copy-start.10
  2.7 0.0 copy-start.11
  2.7 0.0 copy-start.12
  2.7 0.0 copy-start.13
  2.7 0.0 copy-start.14
  2.7 0.0 copy-start.15
  2.7 0.0 copy-start.16
  2.8 10.6 %all-to-all-start = ((bf16[32,144,128]{2,1,0:T(8,128)(2,1)}), bf16[32,144,128]{2,1,0:T(8,128)(2,1)S(1)}, u32[]{:S(2)}, u32[]{:S(2)}) async-start(bf16[32,144,128]{2,1,0:T(8,128)(2,1)} %get-tuple-element.8), calls=%async_computation | async-start | bytes 2359296 | tf_op jit(solution)/shard_map/all_to_all | solution.py:240
  13.4 0.0 copy-done.17
  13.4 31.0 %all_gather.3 = bf16[2304,128]{1,0:T(8,128)(2,1)S(1)} all-gather(bf16[144,128]{1,0:T(8,128)(2,1)S(1)} %copy-done.17), channel_id=1, replica_groups=mesh['row'=32,'col'=16] {'col'}, dimensions={0}, use_global_device_ids=true | all-gather | bytes 626688 | tf_op jit(solution)/shard_map/all_gather | solution.py:241
  44.4 0.0 all-to-all-done.row_ref
  44.4 0.0 copy-done.3
  44.4 0.0 copy-done.4
  44.4 0.0 copy-done.8
  44.4 0.0 copy-done.9
  44.4 0.0 copy-done.10
  44.4 0.0 copy-done.11
  44.4 0.0 copy-done.12
  44.4 0.0 copy-done.13
  44.5 0.0 copy-done.14
  44.5 0.0 copy-done.15
  44.5 0.0 copy-done.16
  44.5 0.0 copy-start
  44.5 0.0 copy-start.1
  44.5 0.0 copy-start.2
  44.5 0.0 copy-start.5
  44.5 0.0 copy-start.6
  44.5 0.0 copy-start.7
  44.6 4.7 %shard_map.177 = (bf16[3072,128]{1,0:T(8,128)(2,1)}, bf16[16,32,128]{2,1,0:T(8,128)(2,1)S(1)}, bf16[32,16,128]{2,1,0:T(8,128)(2,1)S(1)}, f32[8,128]{1,0:T(8,128)S(1)}) custom-call(s32[24]{0:T(128)S(1)} %copy-done.14, s32[1]{0:T(128)} %bitcast.place_ref, bf16[32,144,128]{2,1,0:T(8,128)(2,1)S(1)} %all-to-all-done.row_ref, bf16[16,144,128]{2,1,0:T(8,128)(2,1)S(1)} %bitcast.7, ...), custom_call_target="tpu_custom_call" | custom-call | flops 2000000000 | bytes 4000000 | tf_op jit(solution)/shard_map/pallas_call | solution.py:245
  49.3 20.9 %all_to_all.15.recv_ref = bf16[32,16,128]{2,1,0:T(8,128)(2,1)S(1)} all-to-all(bf16[32,16,128]{2,1,0:T(8,128)(2,1)S(1)} %get-tuple-element.12), channel_id=1, replica_groups=mesh['row'=32,'col'=16] {'row'}, dimensions={0} | all-to-all | bytes 262144 | tf_op jit(solution)/shard_map/all_to_all | solution.py:276
  70.1 18.3 %all_to_all.16.send_ref = bf16[16,32,128]{2,1,0:T(8,128)(2,1)S(1)} all-to-all(bf16[16,32,128]{2,1,0:T(8,128)(2,1)S(1)} %get-tuple-element.11), channel_id=1, replica_groups=mesh['row'=32,'col'=16] {'col'}, dimensions={0} | all-to-all | bytes 262144 | tf_op jit(solution)/shard_map/all_to_all | solution.py:277
  88.4 0.0 copy-done
  88.4 0.0 copy-done.1
  88.4 0.0 copy-done.2
  88.4 0.0 copy-done.5
  88.4 0.0 copy-done.6
  88.4 0.0 copy-done.7
  88.4 1.4 %shard_map.178 = bf16[128,128]{1,0:T(8,128)(2,1)} custom-call(f32[8,128]{1,0:T(8,128)S(1)} %get-tuple-element.10.owner_ref, bf16[16,32,128]{2,1,0:T(8,128)(2,1)S(1)} %all_to_all.16.send_ref, bf16[32,16,128]{2,1,0:T(8,128)(2,1)S(1)} %all_to_all.15.recv_ref, bf16[128,128]{1,0:T(8,128)(2,1)S(1)} %copy-done, bf16[256,128]{1,0:T(8,128)(2,1)S(1)} %copy-done.1, ...), custom_call_target="tpu_custom_call" | custom-call | tf_op jit(solution)/shard_map/pallas_call | solution.py:278
Async XLA Ops:
  2.6 10.7 %copy-start.17 = (bf16[144,128]{1,0:T(8,128)(2,1)S(1)}, bf16[144,128]{1,0:T(8,128)(2,1)}, u32[]{:S(2)}) copy-start(bf16[144,128]{1,0:T(8,128)(2,1)} %get-tuple-element.9) | copy-start | bytes 110596
  2.6 41.8 %copy-start.3 = (s32[16,32]{1,0:T(8,128)S(1)}, s32[16,32]{1,0:T(8,128)}, u32[]{:S(2)}) copy-start(s32[16,32]{1,0:T(8,128)} %send_list_ref.3) | copy-start | bytes 6148
  2.6 41.8 %copy-start.4 = (s32[32,16]{0,1:T(8,128)S(1)}, s32[32,16]{0,1:T(8,128)}, u32[]{:S(2)}) copy-start(s32[32,16]{0,1:T(8,128)} %param.20) | copy-start | bytes 6148
  2.6 41.8 %copy-start.8 = (bf16[3072,128]{1,0:T(8,128)(2,1)S(1)}, bf16[3072,128]{1,0:T(8,128)(2,1)}, u32[]{:S(2)}) copy-start(bf16[3072,128]{1,0:T(8,128)(2,1)} %edges_ref.1) | copy-start | bytes 2359300
  2.7 41.8 %copy-start.9 = (bf16[384,128]{1,0:T(8,128)(2,1)S(1)}, bf16[384,128]{1,0:T(8,128)(2,1)}, u32[]{:S(2)}) copy-start(bf16[384,128]{1,0:T(8,128)(2,1)} %w_in_ref.2) | copy-start | bytes 294916
  2.7 41.8 %copy-start.10 = (bf16[2,128,128]{2,1,0:T(8,128)(2,1)S(1)}, bf16[2,128,128]{2,1,0:T(8,128)(2,1)}, u32[]{:S(2)}) copy-start(bf16[2,128,128]{2,1,0:T(8,128)(2,1)} %w_out_ref.2) | copy-start | bytes 196612
  2.7 41.7 %copy-start.11 = (s32[24,128]{1,0:T(8,128)S(1)}, s32[24,128]{1,0:T(8,128)}, u32[]{:S(2)}) copy-start(s32[24,128]{1,0:T(8,128)} %send_slot_ref.1) | copy-start | bytes 36868
  2.7 41.7 %copy-start.12 = (s32[24,128]{1,0:T(8,128)S(1)}, s32[24,128]{1,0:T(8,128)}, u32[]{:S(2)}) copy-start(s32[24,128]{1,0:T(8,128)} %recv_slot_ref.1) | copy-start | bytes 36868
  2.7 41.7 %copy-start.13 = (f32[3,128]{1,0:T(4,128)S(1)}, f32[3,128]{1,0:T(4,128)}, u32[]{:S(2)}) copy-start(f32[3,128]{1,0:T(4,128)} %bias_ref.2) | copy-start | bytes 4612
  2.7 41.7 %copy-start.14 = (s32[24]{0:T(128)S(1)}, s32[24]{0:T(128)}, u32[]{:S(2)}) copy-start(s32[24]{0:T(128)} %count_ref.1) | copy-start | bytes 292
  2.7 41.7 %copy-start.15 = (f32[128]{0:T(128)S(1)}, f32[128]{0:T(128)}, u32[]{:S(2)}) copy-start(f32[128]{0:T(128)} %param.27) | copy-start | bytes 1540
  2.7 41.7 %copy-start.16 = (f32[128]{0:T(128)S(1)}, f32[128]{0:T(128)}, u32[]{:S(2)}) copy-start(f32[128]{0:T(128)} %param.28) | copy-start | bytes 1540
  2.8 41.6 %all-to-all-start = ((bf16[32,144,128]{2,1,0:T(8,128)(2,1)}), bf16[32,144,128]{2,1,0:T(8,128)(2,1)S(1)}, u32[]{:S(2)}, u32[]{:S(2)}) async-start(bf16[32,144,128]{2,1,0:T(8,128)(2,1)} %get-tuple-element.8), calls=%async_computation | async-start | bytes 2359296 | tf_op jit(solution)/shard_map/all_to_all | solution.py:240
  44.5 43.9 %copy-start = (bf16[128,128]{1,0:T(8,128)(2,1)S(1)}, bf16[128,128]{1,0:T(8,128)(2,1)}, u32[]{:S(2)}) copy-start(bf16[128,128]{1,0:T(8,128)(2,1)} %nodes_ref.3) | copy-start | bytes 98308
  44.5 43.9 %copy-start.1 = (bf16[256,128]{1,0:T(8,128)(2,1)S(1)}, bf16[256,128]{1,0:T(8,128)(2,1)}, u32[]{:S(2)}) copy-start(bf16[256,128]{1,0:T(8,128)(2,1)} %w_in_ref.3) | copy-start | bytes 196612
  44.5 43.9 %copy-start.2 = (bf16[2,128,128]{2,1,0:T(8,128)(2,1)S(1)}, bf16[2,128,128]{2,1,0:T(8,128)(2,1)}, u32[]{:S(2)}) copy-start(bf16[2,128,128]{2,1,0:T(8,128)(2,1)} %w_out_ref.3) | copy-start | bytes 196612
  44.5 43.9 %copy-start.5 = (f32[3,128]{1,0:T(4,128)S(1)}, f32[3,128]{1,0:T(4,128)}, u32[]{:S(2)}) copy-start(f32[3,128]{1,0:T(4,128)} %bias_ref.3) | copy-start | bytes 4612
  44.5 43.9 %copy-start.6 = (f32[128]{0:T(128)S(1)}, f32[128]{0:T(128)}, u32[]{:S(2)}) copy-start(f32[128]{0:T(128)} %param.32) | copy-start | bytes 1540
  44.5 43.9 %copy-start.7 = (f32[128]{0:T(128)S(1)}, f32[128]{0:T(128)}, u32[]{:S(2)}) copy-start(f32[128]{0:T(128)} %param.33) | copy-start | bytes 1540

commit v4 on v3

--- a/solution.py
+++ b/solution.py
@@ -273,8 +273,9 @@
         edge_gain.reshape(1, width),
         edge_shift.reshape(1, width),
     )
+    send_in = lax.all_to_all(send_part, "col", 0, 0, tiled=True)
+    send_in, recv_part = lax.optimization_barrier((send_in, recv_part))
     recv_in = lax.all_to_all(recv_part, "row", 0, 0, tiled=True)
-    send_in = lax.all_to_all(send_part, "col", 0, 0, tiled=True)
     new_nodes = pl.pallas_call(
         node_kernel,
         out_shape=jax.ShapeDtypeStruct(nodes.shape, BF16),

time: 91.1 us -> 91.6 us (level)
  blocking collectives: 70.1 us -> 71.5 us
    all_to_all x1, blocking collectives: 20.9 us -> 22.1 us  [local(): recv_in = lax.all_to_all(recv_part, 'row', 0, 0, tiled=True)]
where the time goes in v4:
time: 91.6 us; the launch traced here: 91.2 us
  blocking collectives  71.5 us (78%)
  starting transfers between devices  10.6 us (12%)
  Pallas kernels  8.08 us (9%)
    all_gather x1, blocking collectives, local(): lax.all_gather(col_send, 'col', axis=0, tiled=True)  31 us
    all_to_all x1, blocking collectives, local(): recv_in = lax.all_to_all(recv_part, 'row', 0, 0, tiled=True)  22.1 us
    all_to_all x1, blocking collectives, local(): send_in = lax.all_to_all(send_part, 'col', 0, 0, tiled=True)  18.4 us
    all_to_all x1, starting transfers between devices, local(): row_block = lax.all_to_all(row_send, 'row', 0, 0, tiled=True)  10.6 us
    pallas_call x1, Pallas kernels, local(): pl.pallas_call(edge_kernel, out_shape=(jax.ShapeDtypeStruct(edges.shape,...  4.7 us
    pallas_call x1, Pallas kernels, local(): pl.pallas_call(pack_kernel, out_shape=(jax.ShapeDtypeStruct((recv_peers,...  2 us
  transfers between devices with their start and end apart: 1, of which 0 were waited for; matrix products, arithmetic and copies ran while one was open for 0% of the time, Pallas kernels for 0%

profile of v4, /device:TPU:1, one launch (start us, length us, event | category | flops | bytes accessed | tf_op | source)
XLA Modules:
  0.0 91.2 jit_solution(8080186030729441390)
XLA Ops:
  0.6 2.0 %shard_map.176 = (bf16[32,144,128]{2,1,0:T(8,128)(2,1)}, bf16[144,128]{1,0:T(8,128)(2,1)}) custom-call(bf16[128,128]{1,0:T(8,128)(2,1)} %nodes_ref.3, s32[16,32]{1,0:T(8,128)} %send_list_ref.3, s32[16,32]{1,0:T(8,128)} %bitcast.8), custom_call_target="tpu_custom_call" | custom-call | tf_op jit(solution)/shard_map/pallas_call | solution.py:230
  2.6 0.0 copy-start.17
  2.6 0.0 copy-start.3
  2.6 0.0 copy-start.4
  2.6 0.0 copy-start.8
  2.7 0.0 copy-start.9
  2.7 0.0 copy-start.10
  2.7 0.0 copy-start.11
  2.7 0.0 copy-start.12
  2.7 0.0 copy-start.13
  2.7 0.0 copy-start.14
  2.7 0.0 copy-start.15
  2.7 0.0 copy-start.16
  2.8 10.6 %all-to-all-start = ((bf16[32,144,128]{2,1,0:T(8,128)(2,1)}), bf16[32,144,128]{2,1,0:T(8,128)(2,1)S(1)}, u32[]{:S(2)}, u32[]{:S(2)}) async-start(bf16[32,144,128]{2,1,0:T(8,128)(2,1)} %get-tuple-element.10), calls=%async_computation | async-start | bytes 2359296 | tf_op jit(solution)/shard_map/all_to_all | solution.py:240
  13.4 0.0 copy-done.17
  13.4 31.0 %all_gather.3 = bf16[2304,128]{1,0:T(8,128)(2,1)S(1)} all-gather(bf16[144,128]{1,0:T(8,128)(2,1)S(1)} %copy-done.17), channel_id=1, replica_groups=mesh['row'=32,'col'=16] {'col'}, dimensions={0}, use_global_device_ids=true | all-gather | bytes 626688 | tf_op jit(solution)/shard_map/all_gather | solution.py:241
  44.4 0.0 all-to-all-done.row_ref
  44.4 0.0 copy-done.3
  44.4 0.0 copy-done.4
  44.4 0.0 copy-done.8
  44.4 0.0 copy-done.9
  44.4 0.0 copy-done.10
  44.4 0.0 copy-done.11
  44.4 0.0 copy-done.12
  44.4 0.0 copy-done.13
  44.5 0.0 copy-done.14
  44.5 0.0 copy-done.15
  44.5 0.0 copy-done.16
  44.5 0.0 copy-start
  44.5 0.0 copy-start.1
  44.5 0.0 copy-start.2
  44.5 0.0 copy-start.5
  44.5 0.0 copy-start.6
  44.5 0.0 copy-start.7
  44.6 4.7 %shard_map.177 = (bf16[3072,128]{1,0:T(8,128)(2,1)}, bf16[16,32,128]{2,1,0:T(8,128)(2,1)S(1)}, bf16[32,16,128]{2,1,0:T(8,128)(2,1)S(1)}, f32[8,128]{1,0:T(8,128)S(1)}) custom-call(s32[24]{0:T(128)S(1)} %copy-done.14, s32[1]{0:T(128)} %bitcast.place_ref, bf16[32,144,128]{2,1,0:T(8,128)(2,1)S(1)} %all-to-all-done.row_ref, bf16[16,144,128]{2,1,0:T(8,128)(2,1)S(1)} %bitcast.7, ...), custom_call_target="tpu_custom_call" | custom-call | flops 2000000000 | bytes 4000000 | tf_op jit(solution)/shard_map/pallas_call | solution.py:245
  49.3 18.4 %all_to_all.15.send_ref = bf16[16,32,128]{2,1,0:T(8,128)(2,1)S(1)} all-to-all(bf16[16,32,128]{2,1,0:T(8,128)(2,1)S(1)} %get-tuple-element.13), channel_id=1, replica_groups=mesh['row'=32,'col'=16] {'col'}, dimensions={0} | all-to-all | bytes 262144 | tf_op jit(solution)/shard_map/all_to_all | solution.py:276
  67.7 22.1 %all_to_all.16.recv_ref = bf16[32,16,128]{2,1,0:T(8,128)(2,1)S(1)} all-to-all(bf16[32,16,128]{2,1,0:T(8,128)(2,1)S(1)} %get-tuple-element.16), channel_id=1, replica_groups=mesh['row'=32,'col'=16] {'row'}, dimensions={0} | all-to-all | bytes 262144 | tf_op jit(solution)/shard_map/all_to_all | solution.py:278
  89.8 0.0 copy-done
  89.8 0.0 copy-done.1
  89.8 0.0 copy-done.2
  89.8 0.0 copy-done.5
  89.8 0.0 copy-done.6
  89.8 0.0 copy-done.7
  89.8 1.4 %shard_map.178 = bf16[128,128]{1,0:T(8,128)(2,1)} custom-call(f32[8,128]{1,0:T(8,128)S(1)} %get-tuple-element.12.owner_ref, bf16[16,32,128]{2,1,0:T(8,128)(2,1)S(1)} %all_to_all.15.send_ref, bf16[32,16,128]{2,1,0:T(8,128)(2,1)S(1)} %all_to_all.16.recv_ref, bf16[128,128]{1,0:T(8,128)(2,1)S(1)} %copy-done, bf16[256,128]{1,0:T(8,128)(2,1)S(1)} %copy-done.1, ...), custom_call_target="tpu_custom_call" | custom-call | tf_op jit(solution)/shard_map/pallas_call | solution.py:279
Async XLA Ops:
  2.6 10.7 %copy-start.17 = (bf16[144,128]{1,0:T(8,128)(2,1)S(1)}, bf16[144,128]{1,0:T(8,128)(2,1)}, u32[]{:S(2)}) copy-start(bf16[144,128]{1,0:T(8,128)(2,1)} %get-tuple-element.11) | copy-start | bytes 110596
  2.6 41.8 %copy-start.3 = (s32[16,32]{1,0:T(8,128)S(1)}, s32[16,32]{1,0:T(8,128)}, u32[]{:S(2)}) copy-start(s32[16,32]{1,0:T(8,128)} %send_list_ref.3) | copy-start | bytes 6148
  2.6 41.8 %copy-start.4 = (s32[32,16]{0,1:T(8,128)S(1)}, s32[32,16]{0,1:T(8,128)}, u32[]{:S(2)}) copy-start(s32[32,16]{0,1:T(8,128)} %param.20) | copy-start | bytes 6148
  2.6 41.8 %copy-start.8 = (bf16[3072,128]{1,0:T(8,128)(2,1)S(1)}, bf16[3072,128]{1,0:T(8,128)(2,1)}, u32[]{:S(2)}) copy-start(bf16[3072,128]{1,0:T(8,128)(2,1)} %edges_ref.1) | copy-start | bytes 2359300
  2.7 41.8 %copy-start.9 = (bf16[384,128]{1,0:T(8,128)(2,1)S(1)}, bf16[384,128]{1,0:T(8,128)(2,1)}, u32[]{:S(2)}) copy-start(bf16[384,128]{1,0:T(8,128)(2,1)} %w_in_ref.2) | copy-start | bytes 294916
  2.7 41.8 %copy-start.10 = (bf16[2,128,128]{2,1,0:T(8,128)(2,1)S(1)}, bf16[2,128,128]{2,1,0:T(8,128)(2,1)}, u32[]{:S(2)}) copy-start(bf16[2,128,128]{2,1,0:T(8,128)(2,1)} %w_out_ref.2) | copy-start | bytes 196612
  2.7 41.7 %copy-start.11 = (s32[24,128]{1,0:T(8,128)S(1)}, s32[24,128]{1,0:T(8,128)}, u32[]{:S(2)}) copy-start(s32[24,128]{1,0:T(8,128)} %send_slot_ref.1) | copy-start | bytes 36868
  2.7 41.7 %copy-start.12 = (s32[24,128]{1,0:T(8,128)S(1)}, s32[24,128]{1,0:T(8,128)}, u32[]{:S(2)}) copy-start(s32[24,128]{1,0:T(8,128)} %recv_slot_ref.1) | copy-start | bytes 36868
  2.7 41.7 %copy-start.13 = (f32[3,128]{1,0:T(4,128)S(1)}, f32[3,128]{1,0:T(4,128)}, u32[]{:S(2)}) copy-start(f32[3,128]{1,0:T(4,128)} %bias_ref.2) | copy-start | bytes 4612
  2.7 41.7 %copy-start.14 = (s32[24]{0:T(128)S(1)}, s32[24]{0:T(128)}, u32[]{:S(2)}) copy-start(s32[24]{0:T(128)} %count_ref.1) | copy-start | bytes 292
  2.7 41.7 %copy-start.15 = (f32[128]{0:T(128)S(1)}, f32[128]{0:T(128)}, u32[]{:S(2)}) copy-start(f32[128]{0:T(128)} %param.27) | copy-start | bytes 1540
  2.7 41.7 %copy-start.16 = (f32[128]{0:T(128)S(1)}, f32[128]{0:T(128)}, u32[]{:S(2)}) copy-start(f32[128]{0:T(128)} %param.28) | copy-start | bytes 1540
  2.8 41.6 %all-to-all-start = ((bf16[32,144,128]{2,1,0:T(8,128)(2,1)}), bf16[32,144,128]{2,1,0:T(8,128)(2,1)S(1)}, u32[]{:S(2)}, u32[]{:S(2)}) async-start(bf16[32,144,128]{2,1,0:T(8,128)(2,1)} %get-tuple-element.10), calls=%async_computation | async-start | bytes 2359296 | tf_op jit(solution)/shard_map/all_to_all | solution.py:240
  44.5 45.3 %copy-start = (bf16[128,128]{1,0:T(8,128)(2,1)S(1)}, bf16[128,128]{1,0:T(8,128)(2,1)}, u32[]{:S(2)}) copy-start(bf16[128,128]{1,0:T(8,128)(2,1)} %nodes_ref.3) | copy-start | bytes 98308
  44.5 45.3 %copy-start.1 = (bf16[256,128]{1,0:T(8,128)(2,1)S(1)}, bf16[256,128]{1,0:T(8,128)(2,1)}, u32[]{:S(2)}) copy-start(bf16[256,128]{1,0:T(8,128)(2,1)} %w_in_ref.3) | copy-start | bytes 196612
  44.5 45.3 %copy-start.2 = (bf16[2,128,128]{2,1,0:T(8,128)(2,1)S(1)}, bf16[2,128,128]{2,1,0:T(8,128)(2,1)}, u32[]{:S(2)}) copy-start(bf16[2,128,128]{2,1,0:T(8,128)(2,1)} %w_out_ref.3) | copy-start | bytes 196612
  44.5 45.3 %copy-start.5 = (f32[3,128]{1,0:T(4,128)S(1)}, f32[3,128]{1,0:T(4,128)}, u32[]{:S(2)}) copy-start(f32[3,128]{1,0:T(4,128)} %bias_ref.3) | copy-start | bytes 4612
  44.5 45.3 %copy-start.6 = (f32[128]{0:T(128)S(1)}, f32[128]{0:T(128)}, u32[]{:S(2)}) copy-start(f32[128]{0:T(128)} %param.32) | copy-start | bytes 1540
  44.5 45.3 %copy-start.7 = (f32[128]{0:T(128)S(1)}, f32[128]{0:T(128)}, u32[]{:S(2)}) copy-start(f32[128]{0:T(128)} %param.33) | copy-start | bytes 1540

commit v5 on v3

--- a/solution.py
+++ b/solution.py
@@ -146,8 +146,8 @@
     proj = jnp.concatenate([send_proj, recv_proj], axis=1)
     edge = edges_ref[...]
     hidden = mm(proj, hot) + mm(edge_w, edge, NT)
-    hidden = jnp.maximum(hidden + b0, 0.0).astype(BF16)
-    hidden = jnp.maximum(mm(mid_w, hidden) + b1, 0.0).astype(BF16)
+    hidden = jnp.maximum((hidden + b0).astype(BF16), BF16(0))
+    hidden = jnp.maximum((mm(mid_w, hidden) + b1).astype(BF16), BF16(0))
     output = mm(last_w, hidden) + b2
     mean = jnp.sum(output, axis=0, keepdims=True) * (1.0 / width)
     centred = output - mean

time: 91.1 us -> 91.1 us (level)
  no operation moved by 1% of the time
where the time goes in v5:
time: 91.1 us; the launch traced here: 89.8 us
  blocking collectives  70.1 us (77%)
  starting transfers between devices  10.6 us (12%)
  Pallas kernels  8.09 us (9%)
    all_gather x1, blocking collectives, local(): lax.all_gather(col_send, 'col', axis=0, tiled=True)  31 us
    all_to_all x1, blocking collectives, local(): recv_in = lax.all_to_all(recv_part, 'row', 0, 0, tiled=True)  20.9 us
    all_to_all x1, blocking collectives, local(): send_in = lax.all_to_all(send_part, 'col', 0, 0, tiled=True)  18.3 us
    all_to_all x1, starting transfers between devices, local(): row_block = lax.all_to_all(row_send, 'row', 0, 0, tiled=True)  10.6 us
    pallas_call x1, Pallas kernels, local(): pl.pallas_call(edge_kernel, out_shape=(jax.ShapeDtypeStruct(edges.shape,...  4.71 us
    pallas_call x1, Pallas kernels, local(): pl.pallas_call(pack_kernel, out_shape=(jax.ShapeDtypeStruct((recv_peers,...  2 us
  transfers between devices with their start and end apart: 1, of which 0 were waited for; matrix products, arithmetic and copies ran while one was open for 0% of the time, Pallas kernels for 0%

profile of v5, /device:TPU:1, one launch (start us, length us, event | category | flops | bytes accessed | tf_op | source)
XLA Modules:
  0.0 89.8 jit_solution(15938244230228148039)
XLA Ops:
  0.6 2.0 %shard_map.176 = (bf16[32,144,128]{2,1,0:T(8,128)(2,1)}, bf16[144,128]{1,0:T(8,128)(2,1)}) custom-call(bf16[128,128]{1,0:T(8,128)(2,1)} %nodes_ref.3, s32[16,32]{1,0:T(8,128)} %send_list_ref.3, s32[16,32]{1,0:T(8,128)} %bitcast.8), custom_call_target="tpu_custom_call" | custom-call | tf_op jit(solution)/shard_map/pallas_call | solution.py:230
  2.6 0.0 copy-start.17
  2.6 0.0 copy-start.3
  2.6 0.0 copy-start.4
  2.6 0.0 copy-start.8
  2.7 0.0 copy-start.9
  2.7 0.0 copy-start.10
  2.7 0.0 copy-start.11
  2.7 0.0 copy-start.12
  2.7 0.0 copy-start.13
  2.7 0.0 copy-start.14
  2.7 0.0 copy-start.15
  2.7 0.0 copy-start.16
  2.8 10.6 %all-to-all-start = ((bf16[32,144,128]{2,1,0:T(8,128)(2,1)}), bf16[32,144,128]{2,1,0:T(8,128)(2,1)S(1)}, u32[]{:S(2)}, u32[]{:S(2)}) async-start(bf16[32,144,128]{2,1,0:T(8,128)(2,1)} %get-tuple-element.8), calls=%async_computation | async-start | bytes 2359296 | tf_op jit(solution)/shard_map/all_to_all | solution.py:240
  13.4 0.0 copy-done.17
  13.4 31.0 %all_gather.3 = bf16[2304,128]{1,0:T(8,128)(2,1)S(1)} all-gather(bf16[144,128]{1,0:T(8,128)(2,1)S(1)} %copy-done.17), channel_id=1, replica_groups=mesh['row'=32,'col'=16] {'col'}, dimensions={0}, use_global_device_ids=true | all-gather | bytes 626688 | tf_op jit(solution)/shard_map/all_gather | solution.py:241
  44.4 0.0 all-to-all-done.row_ref
  44.4 0.0 copy-done.3
  44.4 0.0 copy-done.4
  44.4 0.0 copy-done.8
  44.4 0.0 copy-done.9
  44.4 0.0 copy-done.10
  44.4 0.0 copy-done.11
  44.4 0.0 copy-done.12
  44.4 0.0 copy-done.13
  44.5 0.0 copy-done.14
  44.5 0.0 copy-done.15
  44.5 0.0 copy-done.16
  44.5 0.0 copy-start
  44.5 0.0 copy-start.1
  44.5 0.0 copy-start.2
  44.5 0.0 copy-start.5
  44.5 0.0 copy-start.6
  44.5 0.0 copy-start.7
  44.6 4.7 %shard_map.177 = (bf16[3072,128]{1,0:T(8,128)(2,1)}, bf16[16,32,128]{2,1,0:T(8,128)(2,1)S(1)}, bf16[32,16,128]{2,1,0:T(8,128)(2,1)S(1)}, f32[8,128]{1,0:T(8,128)S(1)}) custom-call(s32[24]{0:T(128)S(1)} %copy-done.14, s32[1]{0:T(128)} %bitcast.place_ref, bf16[32,144,128]{2,1,0:T(8,128)(2,1)S(1)} %all-to-all-done.row_ref, bf16[16,144,128]{2,1,0:T(8,128)(2,1)S(1)} %bitcast.7, ...), custom_call_target="tpu_custom_call" | custom-call | flops 2000000000 | bytes 4000000 | tf_op jit(solution)/shard_map/pallas_call | solution.py:245
  49.3 20.9 %all_to_all.15.recv_ref = bf16[32,16,128]{2,1,0:T(8,128)(2,1)S(1)} all-to-all(bf16[32,16,128]{2,1,0:T(8,128)(2,1)S(1)} %get-tuple-element.12), channel_id=1, replica_groups=mesh['row'=32,'col'=16] {'row'}, dimensions={0} | all-to-all | bytes 262144 | tf_op jit(solution)/shard_map/all_to_all | solution.py:276
  70.1 18.3 %all_to_all.16.send_ref = bf16[16,32,128]{2,1,0:T(8,128)(2,1)S(1)} all-to-all(bf16[16,32,128]{2,1,0:T(8,128)(2,1)S(1)} %get-tuple-element.11), channel_id=1, replica_groups=mesh['row'=32,'col'=16] {'col'}, dimensions={0} | all-to-all | bytes 262144 | tf_op jit(solution)/shard_map/all_to_all | solution.py:277
  88.4 0.0 copy-done
  88.4 0.0 copy-done.1
  88.4 0.0 copy-done.2
  88.4 0.0 copy-done.5
  88.4 0.0 copy-done.6
  88.4 0.0 copy-done.7
  88.4 1.4 %shard_map.178 = bf16[128,128]{1,0:T(8,128)(2,1)} custom-call(f32[8,128]{1,0:T(8,128)S(1)} %get-tuple-element.10.owner_ref, bf16[16,32,128]{2,1,0:T(8,128)(2,1)S(1)} %all_to_all.16.send_ref, bf16[32,16,128]{2,1,0:T(8,128)(2,1)S(1)} %all_to_all.15.recv_ref, bf16[128,128]{1,0:T(8,128)(2,1)S(1)} %copy-done, bf16[256,128]{1,0:T(8,128)(2,1)S(1)} %copy-done.1, ...), custom_call_target="tpu_custom_call" | custom-call | tf_op jit(solution)/shard_map/pallas_call | solution.py:278
Async XLA Ops:
  2.6 10.7 %copy-start.17 = (bf16[144,128]{1,0:T(8,128)(2,1)S(1)}, bf16[144,128]{1,0:T(8,128)(2,1)}, u32[]{:S(2)}) copy-start(bf16[144,128]{1,0:T(8,128)(2,1)} %get-tuple-element.9) | copy-start | bytes 110596
  2.6 41.8 %copy-start.3 = (s32[16,32]{1,0:T(8,128)S(1)}, s32[16,32]{1,0:T(8,128)}, u32[]{:S(2)}) copy-start(s32[16,32]{1,0:T(8,128)} %send_list_ref.3) | copy-start | bytes 6148
  2.6 41.8 %copy-start.4 = (s32[32,16]{0,1:T(8,128)S(1)}, s32[32,16]{0,1:T(8,128)}, u32[]{:S(2)}) copy-start(s32[32,16]{0,1:T(8,128)} %param.20) | copy-start | bytes 6148
  2.6 41.8 %copy-start.8 = (bf16[3072,128]{1,0:T(8,128)(2,1)S(1)}, bf16[3072,128]{1,0:T(8,128)(2,1)}, u32[]{:S(2)}) copy-start(bf16[3072,128]{1,0:T(8,128)(2,1)} %edges_ref.1) | copy-start | bytes 2359300
  2.7 41.8 %copy-start.9 = (bf16[384,128]{1,0:T(8,128)(2,1)S(1)}, bf16[384,128]{1,0:T(8,128)(2,1)}, u32[]{:S(2)}) copy-start(bf16[384,128]{1,0:T(8,128)(2,1)} %w_in_ref.2) | copy-start | bytes 294916
  2.7 41.8 %copy-start.10 = (bf16[2,128,128]{2,1,0:T(8,128)(2,1)S(1)}, bf16[2,128,128]{2,1,0:T(8,128)(2,1)}, u32[]{:S(2)}) copy-start(bf16[2,128,128]{2,1,0:T(8,128)(2,1)} %w_out_ref.2) | copy-start | bytes 196612
  2.7 41.7 %copy-start.11 = (s32[24,128]{1,0:T(8,128)S(1)}, s32[24,128]{1,0:T(8,128)}, u32[]{:S(2)}) copy-start(s32[24,128]{1,0:T(8,128)} %send_slot_ref.1) | copy-start | bytes 36868
  2.7 41.7 %copy-start.12 = (s32[24,128]{1,0:T(8,128)S(1)}, s32[24,128]{1,0:T(8,128)}, u32[]{:S(2)}) copy-start(s32[24,128]{1,0:T(8,128)} %recv_slot_ref.1) | copy-start | bytes 36868
  2.7 41.7 %copy-start.13 = (f32[3,128]{1,0:T(4,128)S(1)}, f32[3,128]{1,0:T(4,128)}, u32[]{:S(2)}) copy-start(f32[3,128]{1,0:T(4,128)} %bias_ref.2) | copy-start | bytes 4612
  2.7 41.7 %copy-start.14 = (s32[24]{0:T(128)S(1)}, s32[24]{0:T(128)}, u32[]{:S(2)}) copy-start(s32[24]{0:T(128)} %count_ref.1) | copy-start | bytes 292
  2.7 41.7 %copy-start.15 = (f32[128]{0:T(128)S(1)}, f32[128]{0:T(128)}, u32[]{:S(2)}) copy-start(f32[128]{0:T(128)} %param.27) | copy-start | bytes 1540
  2.7 41.7 %copy-start.16 = (f32[128]{0:T(128)S(1)}, f32[128]{0:T(128)}, u32[]{:S(2)}) copy-start(f32[128]{0:T(128)} %param.28) | copy-start | bytes 1540
  2.8 41.6 %all-to-all-start = ((bf16[32,144,128]{2,1,0:T(8,128)(2,1)}), bf16[32,144,128]{2,1,0:T(8,128)(2,1)S(1)}, u32[]{:S(2)}, u32[]{:S(2)}) async-start(bf16[32,144,128]{2,1,0:T(8,128)(2,1)} %get-tuple-element.8), calls=%async_computation | async-start | bytes 2359296 | tf_op jit(solution)/shard_map/all_to_all | solution.py:240
  44.5 43.9 %copy-start = (bf16[128,128]{1,0:T(8,128)(2,1)S(1)}, bf16[128,128]{1,0:T(8,128)(2,1)}, u32[]{:S(2)}) copy-start(bf16[128,128]{1,0:T(8,128)(2,1)} %nodes_ref.3) | copy-start | bytes 98308
  44.5 43.9 %copy-start.1 = (bf16[256,128]{1,0:T(8,128)(2,1)S(1)}, bf16[256,128]{1,0:T(8,128)(2,1)}, u32[]{:S(2)}) copy-start(bf16[256,128]{1,0:T(8,128)(2,1)} %w_in_ref.3) | copy-start | bytes 196612
  44.5 43.9 %copy-start.2 = (bf16[2,128,128]{2,1,0:T(8,128)(2,1)S(1)}, bf16[2,128,128]{2,1,0:T(8,128)(2,1)}, u32[]{:S(2)}) copy-start(bf16[2,128,128]{2,1,0:T(8,128)(2,1)} %w_out_ref.3) | copy-start | bytes 196612
  44.5 43.9 %copy-start.5 = (f32[3,128]{1,0:T(4,128)S(1)}, f32[3,128]{1,0:T(4,128)}, u32[]{:S(2)}) copy-start(f32[3,128]{1,0:T(4,128)} %bias_ref.3) | copy-start | bytes 4612
  44.5 43.9 %copy-start.6 = (f32[128]{0:T(128)S(1)}, f32[128]{0:T(128)}, u32[]{:S(2)}) copy-start(f32[128]{0:T(128)} %param.32) | copy-start | bytes 1540
  44.5 43.9 %copy-start.7 = (f32[128]{0:T(128)S(1)}, f32[128]{0:T(128)}, u32[]{:S(2)}) copy-start(f32[128]{0:T(128)} %param.33) | copy-start | bytes 1540
